TPU v7x, 128 devices: a whole 4x4x4 slice. The times are simulated.
128 devices in a mesh: side: 2 (over core), dev: 64 (over y, z, x).
Axes of the slice: x: 4, y: 4, z: 4, core: 2. Of those that a mesh axis runs over, the one named last changes fastest.
Arguments:
- query: bfloat16 [1024, 8, 128], P('dev', 'side'), may hold values from -6 to 6
- key_in: bfloat16 [1024, 8, 128], P('dev', 'side'), may hold values from -6 to 6
- value: bfloat16 [1024, 16, 128], P('dev', 'side'), may hold values from -6 to 6
- out_gate: bfloat16 [1024, 16, 128], P('dev', 'side'), may hold values from -6 to 6
- decay_arg: float32 [1024, 16], P('dev', 'side'), may hold values from -6 to 6
- beta_arg: float32 [1024, 16], P('dev', 'side'), may hold values from -8 to 8
- decay_log: float32 [16], P('side'), may hold values from -3 to 1
- step_bias: float32 [16], P('side'), may hold values from -2 to 1
- states: float32 [1024, 16, 128, 128], P('dev', 'side'), may hold values from -6 to 6
- norm_gain: float32 [128], replicated, may hold values from 0.25 to 1.75
- out_weight: bfloat16 [2048, 2048], P('side'), may hold values from -0.125 to 0.125
- residual: bfloat16 [1024, 2048], P('dev'), may hold values from -3 to 3
- post_gain: float32 [2048], replicated, may hold values from 0.25 to 1.75
- route_ids: int32 [1024, 10], P('dev'), may hold values from 0 to 255, all different within a row; in each aligned block of 16 rows (0 to 15, 16 to 31, ...) at most 3 rows name the same one
- route_weight: float32 [1024, 10], P('dev'), may hold values from 0.05 to 0.5
- w_gate: bfloat16 [256, 2048, 512], P(('side', 'dev')), may hold values from -0.125 to 0.125
- w_up: bfloat16 [256, 2048, 512], P(('side', 'dev')), may hold values from -0.125 to 0.125
- w_down: bfloat16 [256, 512, 2048], P(('side', 'dev')), may hold values from -0.25 to 0.25
Outputs:
- mixed: bfloat16 [1024, 2048], P('dev', 'side')
Inputs may be any that keep to these rules, and one draw needn't show every extreme that they name: `route_ids`: A token's 10 experts are distinct; among the 16 tokens of one index of dev, no expert is named more than 3 times.
All inputs are finite; a program needn't handle non-finite values.
Results may differ from a plain program's by a relative error of at most 0.0059.
Values may be sent and summed in bfloat16 or wider, within the bound.
No kernel may reach another device: no remote copies, remote signals or barrier semaphores. Data moves between devices by JAX's collectives and lax.ppermute only.
A program may use at most 128 MiB of HBM per device.

v0:
```python
import jax
import jax.numpy as jnp
from jax import lax
from jax.sharding import PartitionSpec as P

CAP = 3


EPSILON = 1e-06
TOP_PREC = lax.Precision.HIGHEST


def unit_rows(source):
    source = source.astype(jnp.float32)
    return source * lax.rsqrt(jnp.sum(source * source, -1, keepdims=True) + EPSILON)


def delta_heads(
    query, key_in, value, out_gate, decay_arg, beta_arg, decay_log, step_bias, states, norm_gain
):
    repeats = value.shape[1] // query.shape[1]
    query_unit = jnp.repeat(unit_rows(query), repeats, axis=1) * query.shape[2] ** (-0.5)
    key_unit = jnp.repeat(unit_rows(key_in), repeats, axis=1)
    retain = jnp.exp(-jnp.exp(decay_log) * jax.nn.softplus(decay_arg + step_bias))
    write_rate = jax.nn.sigmoid(beta_arg)
    kstate = jnp.einsum("thi,thij->thj", key_unit, states, precision=TOP_PREC)
    qstate = jnp.einsum("thi,thij->thj", query_unit, states, precision=TOP_PREC)
    correct = write_rate[..., None] * (value.astype(jnp.float32) - retain[..., None] * kstate)
    attend = (
        retain[..., None] * qstate + jnp.sum(query_unit * key_unit, -1, keepdims=True) * correct
    )
    inv_rms = lax.rsqrt(jnp.mean(attend * attend, -1, keepdims=True) + EPSILON)
    gated_out = attend * inv_rms * norm_gain * jax.nn.silu(out_gate.astype(jnp.float32))
    return gated_out.astype(jnp.bfloat16).reshape(value.shape[0], value.shape[1] * value.shape[2])


def slot_table(route_ids, route_weight, side_value, per_side):
    local_ids = route_ids - side_value * per_side
    on_side = (local_ids >= 0) & (local_ids < per_side)
    flat_ids = local_ids.reshape(-1)
    flat_on = on_side.reshape(-1)
    entries = flat_ids.shape[0]
    earlier = lax.broadcasted_iota(jnp.int32, (entries, entries), 0) > lax.broadcasted_iota(
        jnp.int32, (entries, entries), 1
    )
    same_id = (flat_ids[:, None] == flat_ids[None, :]) & earlier & flat_on[None, :]
    position = jnp.sum(same_id.astype(jnp.int32), axis=1)
    slot_index = flat_ids * CAP + position
    slot_hit = (
        slot_index[:, None] == lax.broadcasted_iota(jnp.int32, (entries, per_side * CAP), 1)
    ) & flat_on[:, None]
    slot_hit = slot_hit.astype(jnp.float32).reshape(
        route_ids.shape[0], route_ids.shape[1], per_side * CAP
    )
    picked = jnp.sum(slot_hit, axis=1)
    weights = jnp.einsum("tk,tks->ts", route_weight, slot_hit, precision=TOP_PREC)
    return (picked, weights)


def body(
    query,
    key_in,
    value,
    out_gate,
    decay_arg,
    beta_arg,
    decay_log,
    step_bias,
    states,
    norm_gain,
    out_weight,
    residual,
    post_gain,
    route_ids,
    route_weight,
    w_gate,
    w_up,
    w_down,
):
    gated_out = delta_heads(
        query, key_in, value, out_gate, decay_arg, beta_arg, decay_log, step_bias, states, norm_gain
    )
    partial_value = jnp.dot(gated_out, out_weight, preferred_element_type=jnp.float32)
    model_width = residual.shape[1]
    side_count = lax.axis_size("side")
    dev_count = lax.axis_size("dev")
    half_width = model_width // side_count
    side_index = lax.axis_index("side")
    offset = side_index * half_width
    hidden = residual.astype(jnp.float32) + lax.psum(partial_value, "side")
    inv_rms = lax.rsqrt(jnp.mean(hidden * hidden, -1, keepdims=True) + EPSILON)
    moe_input = (hidden * inv_rms * post_gain).astype(jnp.bfloat16)
    hidden_half = lax.dynamic_slice_in_dim(hidden, offset, half_width, 1)
    expert_count = w_gate.shape[0]
    per_side = dev_count * expert_count
    tables = [
        slot_table(route_ids, route_weight, other_side, per_side)
        for other_side in range(side_count)
    ]
    all_picked = jnp.stack([table[0] for table in tables])
    all_weights = jnp.stack([table[1] for table in tables])
    own_picked = all_picked[side_index]
    send_rows = jnp.dot(
        own_picked.T.astype(jnp.bfloat16), moe_input, preferred_element_type=jnp.float32
    )
    send_rows = send_rows.astype(jnp.bfloat16).reshape(dev_count, expert_count, CAP, model_width)
    received = lax.all_to_all(send_rows, "dev", split_axis=0, concat_axis=0, tiled=True)
    gate_act = jnp.einsum("secd,edf->secf", received, w_gate, preferred_element_type=jnp.float32)
    up_act = jnp.einsum("secd,edf->secf", received, w_up, preferred_element_type=jnp.float32)
    inner = (jax.nn.silu(gate_act) * up_act).astype(jnp.bfloat16)
    expert_out = jnp.einsum(
        "secf,efd->secd", inner, w_down, preferred_element_type=jnp.float32
    ).astype(jnp.bfloat16)
    returned = lax.all_to_all(expert_out, "dev", split_axis=0, concat_axis=0, tiled=True)
    flat_back = returned.reshape(-1, model_width).astype(jnp.float32)
    expert_part = jnp.dot(all_weights[side_index], flat_back, precision=TOP_PREC)
    expert_half = lax.psum_scatter(expert_part, "side", scatter_dimension=1, tiled=True)
    return (hidden_half + expert_half).astype(jnp.bfloat16)


def solution(mesh):
    in_specs = (
        P("dev", "side", None),
        P("dev", "side", None),
        P("dev", "side", None),
        P("dev", "side", None),
        P("dev", "side"),
        P("dev", "side"),
        P("side"),
        P("side"),
        P("dev", "side", None, None),
        P(),
        P("side", None),
        P("dev", None),
        P(),
        P("dev", None),
        P("dev", None),
        P(("side", "dev"), None, None),
        P(("side", "dev"), None, None),
        P(("side", "dev"), None, None),
    )
    out_specs = P("dev", "side")
    return jax.shard_map(body, mesh=mesh, in_specs=in_specs, out_specs=out_specs, check_vma=False)
```

profile of v0, /device:TPU:1, one launch (start us, length us, event | category | flops | bytes accessed | tf_op | source)
XLA Modules:
  0.0 164.8 jit_solution(12976878459039125336)
XLA Ops:
  6.5 0.8 fusion.56
  7.4 0.8 fusion.58
  8.2 0.9 fusion.57
  9.2 10.3 %fusion.78 = f32[16,8,1,128]{3,2,1,0:T(1,128)S(1)} fusion(f32[16,8,128,1]{2,3,1,0:T(1,128)S(1)} %bitcast.91, f32[16,8,128,128]{3,2,1,0:T(8,128)} %param.26), kind=kOutput, calls=%fused_computation.91 | convolution fusion | flops 25165824 | bytes 8519680 | tf_op jit(solution)/shard_map/thi,thij->thj/dot_general | solution.py:26
  19.6 7.3 %fusion.77 = f32[16,8,1,128]{3,2,1,0:T(1,128)S(1)} fusion(f32[16,8,128,1]{2,3,1,0:T(1,128)S(1)} %bitcast.92, f32[16,8,128,128]{3,2,1,0:T(8,128)S(1)} %copy-done.1), kind=kOutput, calls=%fused_computation.90 | convolution fusion | flops 25165824 | bytes 8519680 | tf_op jit(solution)/shard_map/thi,thij->thj/dot_general | solution.py:27
  27.3 0.2 multiply_reduce_fusion.1
  27.6 0.1 fusion.55
  27.7 3.5 %fusion.59 = f32[16,2048]{1,0:T(8,128)} fusion(bf16[1024,2048]{1,0:T(8,128)(2,1)} %param.28, bf16[2,8,8,128]{3,2,1,0:T(8,128)(2,1)S(1)} %bitcast.93), kind=kOutput, calls=%fused_computation.59 | convolution fusion | flops 67108864 | bytes 4358144 | tf_op jit(solution)/shard_map/dot_general | solution.py:83
  31.7 0.2 convert_reduce_fusion.2
  32.0 0.2 convert_reduce_fusion.3
  32.4 0.1 convert_reduce_fusion.1
  32.7 0.1 convert_reduce_fusion
  32.9 25.7 %all-reduce.2.cloned.1.call-done = f32[16,2048]{1,0:T(8,128)} async-done(((f32[16,2048]{1,0:T(8,128)}), f32[16,2048]{1,0:T(8,128)}) %all-reduce.2.cloned.1.call-update) | async-done | bytes 131088 | tf_op jit(solution)/shard_map/psum | solution.py:90
  58.5 1.0 multiply_reduce_fusion
  59.6 1.8 %convolution_convert_fusion = bf16[384,2048]{1,0:T(8,128)(2,1)} fusion(f32[16,2048]{1,0:T(8,128)S(1)} %get-tuple-element.6, f32[2048]{0:T(1024)S(1)} %copy-done.6, f32[16]{0:T(128)S(1)} %add_rsqrt_fusion.3, s32[]{:T(128)S(6)} %select_n.13, bf16[1,16,384]{2,1,0:T(8,128)(2,1)S(1)} %bitcast.95, bf16[1,16,384]{2,1,0:T(8,128)(2,1)S(1)} %bitcast.94), kind=kOutput, calls=%fused_computation.6 | convolution fusion | flops 26056704 | bytes 1736772 | tf_op jit(solution)/shard_map/dot_general | solution.py:103
  61.4 4.0 %reshape.127 = bf16[64,2,3,2048]{3,2,1,0:T(4,128)(2,1)S(1)} reshape(bf16[384,2048]{1,0:T(8,128)(2,1)} %convolution_convert_fusion) | data formatting | bytes 3145728 | tf_op jit(solution)/shard_map/reshape | solution.py:106
  65.4 2.1 %copy.52 = bf16[64,2,3,2048]{3,1,2,0:T(2,128)(2,1)S(1)} copy(bf16[64,2,3,2048]{3,2,1,0:T(4,128)(2,1)S(1)} %reshape.127) | data formatting | bytes 3145728 | tf_op jit(solution)/shard_map/reshape | solution.py:106
  67.5 33.8 %all_to_all.10 = bf16[64,2,3,2048]{3,1,2,0:T(2,128)(2,1)S(1)} all-to-all(bf16[64,2,3,2048]{3,1,2,0:T(2,128)(2,1)S(1)} %copy.52), channel_id=1, replica_groups=mesh['side'=2,'dev'=64] {'dev'}, dimensions={0} | all-to-all | bytes 3145728 | tf_op jit(solution)/shard_map/all_to_all | solution.py:107
  101.3 2.1 %fusion.14 = f32[64,2,3,512]{3,0,2,1:T(8,128)} fusion(bf16[2,2048,512]{2,1,0:T(8,128)(2,1)S(1)} %copy-done.11, bf16[64,2,3,2048]{3,1,2,0:T(2,128)(2,1)S(1)} %all_to_all.10), kind=kOutput, calls=%fused_computation.11 | convolution fusion | flops 805306368 | bytes 6553600 | tf_op jit(solution)/shard_map/secd,edf->secf/dot_general | solution.py:108
  103.5 5.8 %fusion.9 = bf16[64,2,3,2048]{3,0,2,1:T(8,128)(2,1)S(1)} fusion(bf16[2,512,2048]{2,1,0:T(8,128)(2,1)} %param.35, bf16[2,2048,512]{2,1,0:T(8,128)(2,1)} %param.34, bf16[64,2,3,2048]{3,1,2,0:T(2,128)(2,1)S(1)} %all_to_all.10, f32[64,2,3,512]{3,0,2,1:T(8,128)} %fusion.14), kind=kOutput, calls=%fused_computation.8 | convolution fusion | flops 1612578816 | bytes 12320768 | tf_op jit(solution)/shard_map/secf,efd->secd/dot_general | solution.py:111
  109.3 2.8 %copy.55 = bf16[64,2,3,2048]{3,1,2,0:T(2,128)(2,1)} copy(bf16[64,2,3,2048]{3,0,2,1:T(8,128)(2,1)S(1)} %fusion.9) | data formatting | bytes 3145728 | tf_op jit(solution)/shard_map/convert_element_type | solution.py:113
  112.1 5.5 %all-to-all-start.1 = ((bf16[64,2,3,2048]{3,1,2,0:T(2,128)(2,1)}), bf16[64,2,3,2048]{3,1,2,0:T(2,128)(2,1)}, u32[]{:S(2)}, u32[]{:S(2)}) async-start(bf16[64,2,3,2048]{3,1,2,0:T(2,128)(2,1)} %copy.55), calls=%async_computation.1 | async-start | bytes 3145728 | tf_op jit(solution)/shard_map/all_to_all | solution.py:114
  117.6 0.1 fusion.44
  117.7 0.1 fusion.43
  117.9 0.3 fusion.39
  118.2 0.3 fusion.41
  118.5 21.4 %all-to-all-done.1 = bf16[64,2,3,2048]{3,1,2,0:T(2,128)(2,1)} async-done(((bf16[64,2,3,2048]{3,1,2,0:T(2,128)(2,1)}), bf16[64,2,3,2048]{3,1,2,0:T(2,128)(2,1)}, u32[]{:S(2)}, u32[]{:S(2)}) %all-to-all-start.1) | async-done | bytes 1572896 | tf_op jit(solution)/shard_map/all_to_all | solution.py:114
  139.9 2.5 %copy.56 = bf16[64,2,3,2048]{3,2,1,0:T(4,128)(2,1)S(1)} copy(bf16[64,2,3,2048]{3,1,2,0:T(2,128)(2,1)} %all-to-all-done.1) | data formatting | bytes 3145728 | tf_op jit(solution)/shard_map/all_to_all | solution.py:114
  142.4 2.5 %reshape.128 = bf16[384,2048]{1,0:T(8,128)(2,1)} reshape(bf16[64,2,3,2048]{3,2,1,0:T(4,128)(2,1)S(1)} %copy.56) | data formatting | bytes 3145728 | tf_op jit(solution)/shard_map/reshape | solution.py:115
  145.0 2.8 %fusion.66 = f32[16,2048]{1,0:T(8,128)} fusion(bf16[384,2048]{1,0:T(8,128)(2,1)} %reshape.128, s32[]{:T(128)S(6)} %select_n.13, f32[1,16,384]{2,1,0:T(8,128)S(1)} %get-tuple-element.17, f32[1,16,384]{2,1,0:T(8,128)S(1)} %get-tuple-element.16), kind=kOutput, calls=%fused_computation.67 | convolution fusion | flops 151001088 | bytes 1753092 | tf_op jit(solution)/shard_map/dot_general | solution.py:116
  147.8 8.7 %reduce-scatter.2.cloned.1.call-done = f32[16,1024]{1,0:T(8,128)} async-done(((f32[16,2048]{1,0:T(8,128)}), f32[16,1024]{1,0:T(8,128)}) %reduce-scatter.2.cloned.1.call-update) | async-done | bytes 65552 | tf_op jit(solution)/shard_map/reduce_scatter | solution.py:117
  156.5 1.5 add_convert_fusion
  (57 shorter events, 1.5 us)
Async XLA Ops:
  6.5 111.3 %copy-start = (f32[16,10]{1,0:T(8,128)S(1)}, f32[16,10]{1,0:T(8,128)}, u32[]{:S(2)}) copy-start(f32[16,10]{1,0:T(8,128)} %param.32) | copy-start | bytes 1924
  6.5 52.0 %all-reduce.2.cloned.1.call-start = ((), (), s32[]{:S(2)}) async-start(), calls=%async_computation.3 | async-start | bytes 262144 | tf_op jit(solution)/shard_map/psum | solution.py:90
  9.1 10.3 %copy-start.1 = (f32[16,8,128,128]{3,2,1,0:T(8,128)S(1)}, f32[16,8,128,128]{3,2,1,0:T(8,128)}, u32[]{:S(2)}) copy-start(f32[16,8,128,128]{3,2,1,0:T(8,128)} %param.26) | copy-start | bytes 25165828
  19.5 7.5 %copy-start.12 = (f32[8]{0:T(128)S(1)}, f32[8]{0:T(128)}, u32[]{:S(2)}) copy-start(f32[8]{0:T(128)} %param.24) | copy-start | bytes 100
  19.5 7.5 %copy-start.7 = (f32[16,8]{0,1:T(8,128)S(1)}, f32[16,8]{0,1:T(8,128)}, u32[]{:S(2)}) copy-start(f32[16,8]{0,1:T(8,128)} %param.22) | copy-start | bytes 1540
  19.5 7.5 %copy-start.10 = (f32[8]{0:T(128)S(1)}, f32[8]{0:T(128)}, u32[]{:S(2)}) copy-start(f32[8]{0:T(128)} %param.25) | copy-start | bytes 100
  19.5 7.7 %copy-start.8 = (f32[16,8]{0,1:T(8,128)S(1)}, f32[16,8]{0,1:T(8,128)}, u32[]{:S(2)}) copy-start(f32[16,8]{0,1:T(8,128)} %param.23) | copy-start | bytes 1540
  19.6 7.8 %copy-start.3 = (bf16[16,8,128]{2,1,0:T(8,128)(2,1)S(1)}, bf16[16,8,128]{2,1,0:T(8,128)(2,1)}, u32[]{:S(2)}) copy-start(bf16[16,8,128]{2,1,0:T(8,128)(2,1)} %param.20) | copy-start | bytes 98308
  19.6 8.0 %copy-start.5 = (bf16[16,8,128]{2,1,0:T(8,128)(2,1)S(1)}, bf16[16,8,128]{2,1,0:T(8,128)(2,1)}, u32[]{:S(2)}) copy-start(bf16[16,8,128]{2,1,0:T(8,128)(2,1)} %param.21) | copy-start | bytes 98308
  19.6 8.0 %copy-start.9 = (f32[128]{0:T(128)S(1)}, f32[128]{0:T(128)}, u32[]{:S(2)}) copy-start(f32[128]{0:T(128)} %param.27) | copy-start | bytes 1540
  26.9 4.4 %copy-start.2 = (s32[16,10]{1,0:T(8,128)S(1)}, s32[16,10]{1,0:T(8,128)}, u32[]{:S(2)}) copy-start(s32[16,10]{1,0:T(8,128)} %param.31) | copy-start | bytes 1924
  26.9 31.7 %copy-start.4 = (bf16[16,2048]{1,0:T(8,128)(2,1)S(1)}, bf16[16,2048]{1,0:T(8,128)(2,1)}, u32[]{:S(2)}) copy-start(bf16[16,2048]{1,0:T(8,128)(2,1)} %param.29) | copy-start | bytes 196612
  26.9 32.7 %copy-start.6 = (f32[2048]{0:T(1024)S(1)}, f32[2048]{0:T(1024)}, u32[]{:S(2)}) copy-start(f32[2048]{0:T(1024)} %param.30) | copy-start | bytes 24580
  65.4 36.0 %copy-start.11 = (bf16[2,2048,512]{2,1,0:T(8,128)(2,1)S(1)}, bf16[2,2048,512]{2,1,0:T(8,128)(2,1)}, u32[]{:S(2)}) copy-start(bf16[2,2048,512]{2,1,0:T(8,128)(2,1)} %param.33) | copy-start | bytes 12582916
  112.1 27.8 %all-to-all-start.1 = ((bf16[64,2,3,2048]{3,1,2,0:T(2,128)(2,1)}), bf16[64,2,3,2048]{3,1,2,0:T(2,128)(2,1)}, u32[]{:S(2)}, u32[]{:S(2)}) async-start(bf16[64,2,3,2048]{3,1,2,0:T(2,128)(2,1)} %copy.55), calls=%async_computation.1 | async-start | bytes 3145728 | tf_op jit(solution)/shard_map/all_to_all | solution.py:114
  117.6 39.0 %reduce-scatter.2.cloned.1.call-start = ((), (), s32[]{:S(2)}) async-start(), calls=%async_computation.4 | async-start | bytes 196608 | tf_op jit(solution)/shard_map/reduce_scatter | solution.py:117
Sparse Core Ops, SparseCore 0:
  31.4 27.1 all-reduce.1
  147.9 8.5 reduce-scatter.1
where the time goes:
time: 165 us
  waiting for transfers between devices  55.9 us (34%)
  matrix products  34.1 us (21%)
  blocking collectives  33.8 us (20%)
  local copies, waits for them, and re-layouts  15.3 us (9%)
  between operations  13.8 us (8%)
  other arithmetic  6.38 us (4%)
  starting transfers between devices  5.54 us (3%)
    all_to_all x1, blocking collectives, body(): lax.all_to_all(send_rows, 'dev', split_axis=0, concat_axis=0, tiled=True)  33.8 us
    psum x1, waiting for transfers between devices, body(): hidden = residual.astype(jnp.float32) + lax.psum(partial_value, 'side')  25.7 us
    all_to_all x1, waiting for transfers between devices, body(): lax.all_to_all(expert_out, 'dev', split_axis=0, concat_axis=0, tiled=True)  21.4 us
    dot_general x1, matrix products, delta_heads(): kstate = jnp.einsum('thi,thij->thj', key_unit, states, precision=TOP_PREC)  10.3 us
    reduce_scatter x1, waiting for transfers between devices, body(): lax.psum_scatter(expert_part, 'side', scatter_dimension=1, tiled=True)  8.75 us
    dot_general x1, matrix products, delta_heads(): qstate = jnp.einsum('thi,thij->thj', query_unit, states, precision=TOP_PREC)  7.26 us
    reshape x2, local copies, waits for them, and re-layouts, body(): send_rows.astype(jnp.bfloat16)  6.11 us
    dot_general x1, matrix products, body(): jnp.einsum('secf,efd->secd', inner, w_down, preferred_element_type=jnp.fl...  5.84 us
  transfers between devices with their start and end apart: 3, of which 3 were waited for; matrix products, arithmetic and copies ran while one was open for 1% of the time, Pallas kernels for 0%

commit v1 on v0

v1 whole, which is shorter than its diff:
```python
import jax
import jax.numpy as jnp
from jax import lax
from jax.experimental import pallas as pl
from jax.experimental.pallas import tpu as pltpu
from jax.sharding import PartitionSpec as P

CAP = 3
EPSILON = 1e-06
LANES = 128
TILE = 16
STEP_TOKENS = 2
MIB = 1 << 20


def softplus(x):
    return jnp.maximum(x, 0.0) + jnp.log1p(jnp.exp(-jnp.abs(x)))


def sigmoid(x):
    return 1.0 / (1.0 + jnp.exp(-x))


def unit_rows(source):
    return source * lax.rsqrt(jnp.sum(source * source, -1, keepdims=True) + EPSILON)


def row_to_column(row):
    n = row.shape[1]
    square = jnp.broadcast_to(row, (n, n))
    on_diagonal = lax.broadcasted_iota(jnp.int32, (n, n), 0) == lax.broadcasted_iota(
        jnp.int32, (n, n), 1
    )
    return jnp.sum(jnp.where(on_diagonal, square, 0.0), axis=1, keepdims=True)


def pick_column(table, column):
    lane = lax.broadcasted_iota(jnp.int32, table.shape, 1)
    return jnp.sum(jnp.where(lane == column, table, 0.0), axis=1, keepdims=True)


def delta_kernel(
    side_ref,
    query_ref,
    key_ref,
    value_ref,
    gate_ref,
    decay_ref,
    beta_ref,
    log_ref,
    bias_ref,
    state_ref,
    gain_ref,
    residual_ref,
    weight_hbm,
    out_ref,
    weight_ref,
    heads_ref,
    weight_sem,
):
    step = pl.program_id(0)
    steps = pl.num_programs(0)
    tokens, width = residual_ref.shape
    heads = value_ref.shape[1]
    key_heads = query_ref.shape[1]
    repeats = heads // key_heads
    size = query_ref.shape[2]
    load = pltpu.make_async_copy(weight_hbm, weight_ref, weight_sem)

    @pl.when(step == 0)
    def _():
        load.start()

    retain_all = jnp.exp(
        -jnp.exp(row_to_column(log_ref[...]))
        * softplus(decay_ref[...] + row_to_column(bias_ref[...]))
    )
    rate_all = sigmoid(beta_ref[...])
    units = []
    for j in range(STEP_TOKENS):
        units.append(unit_rows(query_ref[j].astype(jnp.float32)) * size ** (-0.5))
        units.append(unit_rows(key_ref[j].astype(jnp.float32)))
    rows = jnp.concatenate(units, 0)
    columns = rows.T
    for j in range(STEP_TOKENS):
        token = step * STEP_TOKENS + j
        query_unit, key_unit = units[2 * j], units[2 * j + 1]
        products = jnp.sum(query_unit * key_unit, -1, keepdims=True)
        qrows, krows, prows = [], [], []
        for k in range(key_heads):
            at = 2 * j * key_heads + k
            qcol = jnp.broadcast_to(columns[:, at : at + 1], (size, size))
            at = at + key_heads
            kcol = jnp.broadcast_to(columns[:, at : at + 1], (size, size))
            for r in range(repeats):
                state = state_ref[j, k * repeats + r]
                qrows.append(jnp.sum(qcol * state, axis=0, keepdims=True))
                krows.append(jnp.sum(kcol * state, axis=0, keepdims=True))
                prows.append(products[k : k + 1])
        qstate = jnp.concatenate(qrows, 0)
        kstate = jnp.concatenate(krows, 0)
        product = jnp.concatenate(prows, 0)
        retain = pick_column(retain_all, token)
        rate = pick_column(rate_all, token)
        correct = rate * (value_ref[j].astype(jnp.float32) - retain * kstate)
        attend = retain * qstate + product * correct
        inv_rms = lax.rsqrt(jnp.mean(attend * attend, -1, keepdims=True) + EPSILON)
        gate = gate_ref[j].astype(jnp.float32)
        gated = attend * inv_rms * gain_ref[...] * (gate * sigmoid(gate))
        heads_ref[pl.ds(pl.multiple_of(token * heads, heads), heads), :] = gated

    @pl.when(step == steps - 1)
    def _():
        gated_out = jnp.concatenate(
            [heads_ref[pl.ds(h, tokens, stride=heads), :] for h in range(heads)], 1
        ).astype(jnp.bfloat16)
        load.wait()
        side = side_ref[0]
        blocks = width // LANES
        wide = 4 * LANES
        for n in range(width // wide):
            part = jnp.dot(
                gated_out,
                weight_ref[:, n * wide : (n + 1) * wide],
                preferred_element_type=jnp.float32,
            )
            kept = residual_ref[:, n * wide : (n + 1) * wide].astype(jnp.float32)
            part = part + jnp.where(side == 0, kept, 0.0)
            for f in range(4):
                out_ref[pl.ds(n * 4 + f, tokens, stride=blocks), :] = part[
                    :, f * LANES : (f + 1) * LANES
                ]


def delta_call(side, query, key_in, value, gate, decay, beta, log, bias, states, gain, residual, weight):
    tokens, heads, size = value.shape
    key_heads = query.shape[1]
    width = residual.shape[1]

    def by_token(*shape):
        return pl.BlockSpec((STEP_TOKENS,) + shape, lambda i: (i,) + (0,) * len(shape))

    def whole(array):
        return pl.BlockSpec(array.shape, lambda i: (0,) * array.ndim)

    return pl.pallas_call(
        delta_kernel,
        grid=(tokens // STEP_TOKENS,),
        out_shape=jax.ShapeDtypeStruct((tokens * width // LANES, LANES), jnp.float32),
        in_specs=[
            pl.BlockSpec(memory_space=pltpu.SMEM),
            by_token(key_heads, size),
            by_token(key_heads, size),
            by_token(heads, size),
            by_token(heads, size),
            whole(decay),
            whole(beta),
            whole(log),
            whole(bias),
            by_token(heads, size, size),
            whole(gain),
            whole(residual),
            pl.BlockSpec(memory_space=pl.ANY),
        ],
        out_specs=pl.BlockSpec((tokens * width // LANES, LANES), lambda i: (0, 0)),
        scratch_shapes=[
            pltpu.VMEM(weight.shape, weight.dtype),
            pltpu.VMEM((tokens * heads, size), jnp.float32),
            pltpu.SemaphoreType.DMA,
        ],
        compiler_params=pltpu.CompilerParams(vmem_limit_bytes=16 * MIB),
        name="delta",
    )(side, query, key_in, value, gate, decay, beta, log, bias, states, gain, residual, weight)


def pack_kernel(source_ref, own_ref, other_ref, gain_ref, out_ref, tiles_ref):
    blocks = gain_ref.shape[0]
    tokens = own_ref.shape[0] // blocks
    for t in range(tokens):
        rows = slice(t * blocks, (t + 1) * blocks)
        hidden = own_ref[rows, :] + other_ref[rows, :]
        mean = jnp.sum(
            jnp.sum(hidden * hidden, axis=0, keepdims=True), axis=1, keepdims=True
        ) * (1.0 / (blocks * LANES))
        tiles_ref[rows, :] = (hidden * lax.rsqrt(mean + EPSILON) * gain_ref[...]).astype(
            jnp.bfloat16
        )
    tiles_ref[tokens * blocks :, :] = jnp.zeros((blocks, LANES), jnp.bfloat16)
    slots = out_ref.shape[0] // blocks
    for s in range(slots):
        at = pl.multiple_of(source_ref[s] * blocks, blocks)
        out_ref[s * blocks : (s + 1) * blocks, :] = tiles_ref[pl.ds(at, blocks), :]


def pack_call(source, own, other, gain):
    blocks = gain.shape[0]
    slots = source.shape[0]
    vmem = pl.BlockSpec(memory_space=pltpu.VMEM)
    return pl.pallas_call(
        pack_kernel,
        out_shape=jax.ShapeDtypeStruct((slots * blocks, LANES), jnp.bfloat16),
        in_specs=[pl.BlockSpec(memory_space=pltpu.SMEM), vmem, vmem, vmem],
        out_specs=vmem,
        scratch_shapes=[pltpu.VMEM((own.shape[0] + blocks, LANES), jnp.bfloat16)],
        compiler_params=pltpu.CompilerParams(vmem_limit_bytes=16 * MIB),
        name="pack",
    )(source, own, other, gain)


def expert_kernel(
    x_ref, gate_hbm, up_hbm, down_hbm, out_ref, gate_ref, up_ref, down_ref, rows_ref, sems
):
    experts, width, units = gate_hbm.shape
    sources = x_ref.shape[0]
    blocks = width // LANES
    groups = sources // TILE
    copies = []
    for e in range(experts):
        for i, (hbm, ref) in enumerate(
            ((gate_hbm, gate_ref), (up_hbm, up_ref), (down_hbm, down_ref))
        ):
            copies.append(pltpu.make_async_copy(hbm.at[e], ref.at[e], sems.at[e, i]))
            copies[-1].start()
    row = lax.broadcasted_iota(jnp.int32, (TILE * blocks, TILE * blocks), 0)
    column = lax.broadcasted_iota(jnp.int32, (TILE * blocks, TILE * blocks), 1)
    swap = jnp.where((row % TILE) * TILE + row // TILE == column, 1.0, 0.0).astype(jnp.bfloat16)
    for e in range(experts):
        for g in range(groups):
            for c in range(CAP):
                at = (e * CAP + c) * blocks
                block = x_ref[g * TILE : (g + 1) * TILE, at : at + blocks, :]
                block = block.reshape(TILE * blocks, LANES)
                turned = jnp.dot(swap, block, preferred_element_type=jnp.float32)
                turned = turned.astype(jnp.bfloat16)
                r = ((e * groups + g) * CAP + c) * TILE
                for f in range(blocks):
                    rows_ref[r : r + TILE, f * LANES : (f + 1) * LANES] = turned[
                        f * TILE : (f + 1) * TILE
                    ]
    count = groups * CAP * TILE
    for e in range(experts):
        x = rows_ref[e * count : (e + 1) * count, :]
        copies[3 * e].wait()
        gate = jnp.dot(x, gate_ref[e], preferred_element_type=jnp.float32)
        copies[3 * e + 1].wait()
        up = jnp.dot(x, up_ref[e], preferred_element_type=jnp.float32)
        inner = (gate * sigmoid(gate) * up).astype(jnp.bfloat16)
        copies[3 * e + 2].wait()
        wide = 4 * LANES
        for n in range(width // wide):
            y = jnp.dot(
                inner, down_ref[e, :, n * wide : (n + 1) * wide], preferred_element_type=jnp.float32
            )
            rows_ref[e * count : (e + 1) * count, n * wide : (n + 1) * wide] = y.astype(
                jnp.bfloat16
            )
        for g in range(groups):
            for c in range(CAP):
                r = ((e * groups + g) * CAP + c) * TILE
                block = jnp.concatenate(
                    [
                        rows_ref[r : r + TILE, f * LANES : (f + 1) * LANES]
                        for f in range(blocks)
                    ],
                    0,
                )
                turned = jnp.dot(swap, block, preferred_element_type=jnp.float32)
                at = (e * CAP + c) * blocks
                out_ref[g * TILE : (g + 1) * TILE, at : at + blocks, :] = turned.astype(
                    jnp.bfloat16
                ).reshape(TILE, blocks, LANES)


def expert_call(received, w_gate, w_up, w_down):
    experts, width, units = w_gate.shape
    vmem = pl.BlockSpec(memory_space=pltpu.VMEM)
    hbm = pl.BlockSpec(memory_space=pl.ANY)
    slots = received.shape[0] * CAP * experts
    return pl.pallas_call(
        expert_kernel,
        out_shape=jax.ShapeDtypeStruct(received.shape, received.dtype),
        in_specs=[vmem, hbm, hbm, hbm],
        out_specs=vmem,
        scratch_shapes=[
            pltpu.VMEM(w_gate.shape, w_gate.dtype),
            pltpu.VMEM(w_up.shape, w_up.dtype),
            pltpu.VMEM(w_down.shape, w_down.dtype),
            pltpu.VMEM((slots, width), jnp.bfloat16),
            pltpu.SemaphoreType.DMA((experts, 3)),
        ],
        compiler_params=pltpu.CompilerParams(vmem_limit_bytes=32 * MIB),
        name="experts",
    )(received, w_gate, w_up, w_down)


def gather_kernel(side_ref, slot_ref, weight_ref, back_ref, keep_ref, send_ref, sums_ref):
    blocks = sums_ref.shape[0]
    half = blocks // 2
    tokens = keep_ref.shape[0] // half
    top = slot_ref.shape[0] // tokens
    side = side_ref[0]
    for t in range(tokens):
        total = jnp.zeros((blocks, LANES), jnp.float32)
        for k in range(top):
            at = pl.multiple_of(slot_ref[t * top + k] * blocks, blocks)
            tile = back_ref[pl.ds(at, blocks), :].astype(jnp.float32)
            total = total + weight_ref[t * top + k] * tile
        sums_ref[...] = total
        own = pl.multiple_of(side * half, half)
        other = pl.multiple_of((1 - side) * half, half)
        keep_ref[t * half : (t + 1) * half, :] = sums_ref[pl.ds(own, half), :]
        send_ref[t * half : (t + 1) * half, :] = sums_ref[pl.ds(other, half), :]


def gather_call(side, slots, weights, back, tokens, blocks):
    vmem = pl.BlockSpec(memory_space=pltpu.VMEM)
    smem = pl.BlockSpec(memory_space=pltpu.SMEM)
    half = jax.ShapeDtypeStruct((tokens * blocks // 2, LANES), jnp.float32)
    return pl.pallas_call(
        gather_kernel,
        out_shape=(half, half),
        in_specs=[smem, smem, smem, vmem],
        out_specs=(vmem, vmem),
        scratch_shapes=[pltpu.VMEM((blocks, LANES), jnp.float32)],
        compiler_params=pltpu.CompilerParams(vmem_limit_bytes=16 * MIB),
        name="combine",
    )(side, slots, weights, back)


def last_kernel(side_ref, own_ref, other_ref, keep_ref, got_ref, out_ref, sums_ref):
    tokens, width = out_ref.shape
    half = width // LANES
    side = side_ref[0]
    for t in range(tokens):
        at = pl.multiple_of((2 * t + side) * half, half)
        rows = slice(t * half, (t + 1) * half)
        hidden = own_ref[pl.ds(at, half), :] + other_ref[pl.ds(at, half), :]
        sums_ref[rows, :] = hidden + (keep_ref[rows, :] + got_ref[rows, :])
    for f in range(half):
        out_ref[:, f * LANES : (f + 1) * LANES] = sums_ref[
            pl.ds(f, tokens, stride=half), :
        ].astype(jnp.bfloat16)


def last_call(side, own, other, keep, got, tokens):
    vmem = pl.BlockSpec(memory_space=pltpu.VMEM)
    return pl.pallas_call(
        last_kernel,
        out_shape=jax.ShapeDtypeStruct((tokens, keep.size // tokens), jnp.bfloat16),
        in_specs=[pl.BlockSpec(memory_space=pltpu.SMEM), vmem, vmem, vmem, vmem],
        out_specs=vmem,
        scratch_shapes=[pltpu.VMEM(keep.shape, jnp.float32)],
        compiler_params=pltpu.CompilerParams(vmem_limit_bytes=16 * MIB),
        name="last",
    )(side, own, other, keep, got)


def slot_tables(route_ids, route_weight, side_index, per_side, experts):
    tokens, top = route_ids.shape
    entries = tokens * top
    ids = route_ids.reshape(-1)
    token = lax.broadcasted_iota(jnp.int32, (tokens, top), 0).reshape(-1)
    same = (ids[:, None] == ids[None, :]) & (token[:, None] > token[None, :])
    position = jnp.sum(same.astype(jnp.int32), axis=1)
    local = ids - side_index * per_side
    on_side = (local >= 0) & (local < per_side)
    slot = jnp.where(on_side, local * CAP + position, -1)
    weights = jnp.where(on_side, route_weight.reshape(-1), 0.0)
    hit = slot[None, :] == lax.broadcasted_iota(jnp.int32, (per_side * CAP, entries), 0)
    source = tokens - jnp.sum(jnp.where(hit, tokens - token[None, :], 0), axis=1)
    return source, jnp.maximum(slot, 0), weights


def body(
    query,
    key_in,
    value,
    out_gate,
    decay_arg,
    beta_arg,
    decay_log,
    step_bias,
    states,
    norm_gain,
    out_weight,
    residual,
    post_gain,
    route_ids,
    route_weight,
    w_gate,
    w_up,
    w_down,
):
    tokens, width = residual.shape
    blocks = width // LANES
    dev_count = lax.axis_size("dev")
    experts = w_gate.shape[0]
    side_index = lax.axis_index("side")
    side = side_index.reshape(1)
    swap = [(0, 1), (1, 0)]
    own = delta_call(
        side,
        query,
        key_in,
        value,
        out_gate,
        decay_arg.T,
        beta_arg.T,
        decay_log.reshape(1, -1),
        step_bias.reshape(1, -1),
        states,
        norm_gain.reshape(1, -1),
        residual,
        out_weight,
    )
    other = lax.ppermute(own, "side", swap)
    source, slots, weights = slot_tables(
        route_ids, route_weight, side_index, dev_count * experts, experts
    )
    send_rows = pack_call(source, own, other, post_gain.reshape(blocks, LANES))
    received = lax.all_to_all(send_rows, "dev", split_axis=0, concat_axis=0, tiled=True)
    expert_out = expert_call(
        received.reshape(dev_count, -1, LANES), w_gate, w_up, w_down
    ).reshape(received.shape)
    back = lax.all_to_all(expert_out, "dev", split_axis=0, concat_axis=0, tiled=True)
    keep, send = gather_call(side, slots, weights, back, tokens, blocks)
    got = lax.ppermute(send, "side", swap)
    return last_call(side, own, other, keep, got, tokens)


def solution(mesh):
    in_specs = (
        P("dev", "side", None),
        P("dev", "side", None),
        P("dev", "side", None),
        P("dev", "side", None),
        P("dev", "side"),
        P("dev", "side"),
        P("side"),
        P("side"),
        P("dev", "side", None, None),
        P(),
        P("side", None),
        P("dev", None),
        P(),
        P("dev", None),
        P("dev", None),
        P(("side", "dev"), None, None),
        P(("side", "dev"), None, None),
        P(("side", "dev"), None, None),
    )
    out_specs = P("dev", "side")
    return jax.shard_map(body, mesh=mesh, in_specs=in_specs, out_specs=out_specs, check_vma=False)
```

time: 165 us -> 104 us (0.63)
  matrix products: 34.1 us -> 0 us
  waiting for transfers between devices: 55.9 us -> 23.7 us
  Pallas kernels: 0 us -> 17.9 us
  between operations: 13.8 us -> 0.11 us
  other arithmetic: 6.38 us -> 0.37 us
  starting transfers between devices: 5.54 us -> 9.46 us
  local copies, waits for them, and re-layouts: 15.3 us -> 17.3 us
    dot_general x9 -> x0, matrix products: 34.1 us -> none  [the longest x1 10.3 us: delta_heads(): kstate = jnp.einsum('thi,thij->thj', key_unit, states, precision=TOP_PREC)]
    psum x1 -> x0, waiting for transfers between devices: 25.7 us -> none  [body(): hidden = residual.astype(jnp.float32) + lax.psum(partial_value, 'side')]
    pallas_call x0 -> x5, Pallas kernels: none -> 17.9 us  [the longest x1 7.72 us: delta_call(): pl.pallas_call(delta_kernel, grid=(tokens // STEP_TOKENS,), out_shape=jax...]
    unnamed x26 -> x36, local copies, waits for them, and re-layouts: 0.07 us -> 17.1 us
    reduce_scatter x1 -> x0, waiting for transfers between devices: 8.75 us -> none  [body(): lax.psum_scatter(expert_part, 'side', scatter_dimension=1, tiled=True)]
    reshape x3 -> x2, local copies, waits for them, and re-layouts: 8.65 us -> 0.17 us  [the longest x1 0.08 us: slot_tables(): weights = jnp.where(on_side, route_weight.reshape(-1), 0.0)]
    ppermute x0 -> x2, starting transfers between devices: none -> 4.53 us  [the longest x1 3.03 us: body(): got = lax.ppermute(send, 'side', swap)]
    reduce_sum x8 -> x2, other arithmetic: 3.49 us -> 0.34 us  [the longest x1 0.21 us: slot_tables(): position = jnp.sum(same.astype(jnp.int32), axis=1)]
where the time goes in v1:
time: 104 us
  blocking collectives  34.7 us (33%)
  waiting for transfers between devices  23.7 us (23%)
  Pallas kernels  17.9 us (17%)
  local copies, waits for them, and re-layouts  17.3 us (17%)
  starting transfers between devices  9.46 us (9%)
    all_to_all x1, blocking collectives, body(): lax.all_to_all(send_rows, 'dev', split_axis=0, concat_axis=0, tiled=True)  34.7 us
    all_to_all x1, waiting for transfers between devices, body(): lax.all_to_all(expert_out, 'dev', split_axis=0, concat_axis=0, tiled=True)  22.4 us
    unnamed x36, local copies, waits for them, and re-layouts  17.1 us
    pallas_call x1, Pallas kernels, delta_call(): pl.pallas_call(delta_kernel, grid=(tokens // STEP_TOKENS,), out_shape=jax...  7.72 us
    pallas_call x1, Pallas kernels, expert_call(): pl.pallas_call(expert_kernel, out_shape=jax.ShapeDtypeStruct(received.sha...  7.6 us
    all_to_all x1, starting transfers between devices, body(): lax.all_to_all(expert_out, 'dev', split_axis=0, concat_axis=0, tiled=True)  4.93 us
    ppermute x1, starting transfers between devices, body(): got = lax.ppermute(send, 'side', swap)  3.03 us
  transfers between devices with their start and end apart: 3, of which 3 were waited for; matrix products, arithmetic and copies ran while one was open for 1% of the time, Pallas kernels for 0%

profile of v1, /device:TPU:1, one launch (start us, length us, event | category | flops | bytes accessed | tf_op | source)
XLA Modules:
  0.0 103.6 jit_solution(249443690350171574)
XLA Ops:
  0.0 3.4 %copy-done = f32[16,8,128,128]{3,2,1,0:T(8,128)S(1)} copy-done((f32[16,8,128,128]{3,2,1,0:T(8,128)S(1)}, f32[16,8,128,128]{3,2,1,0:T(8,128)}, u32[]{:S(2)}) %copy-start) | copy-done | bytes 8388632
  3.4 2.2 %copy-done.1 = bf16[1024,2048]{1,0:T(8,128)(2,1)S(1)} copy-done((bf16[1024,2048]{1,0:T(8,128)(2,1)S(1)}, bf16[1024,2048]{1,0:T(8,128)(2,1)}, u32[]{:S(2)}) %copy-start.1) | copy-done | bytes 4194328
  5.6 0.8 copy-done.5
  6.4 0.8 copy-done.6
  7.2 0.8 copy-done.7
  7.9 0.7 copy-done.8
  8.6 0.7 copy-done.9
  9.4 0.7 copy-done.11
  10.1 0.7 copy-done.12
  10.7 0.7 copy-done.13
  11.4 0.7 copy-done.14
  12.1 0.7 copy-done.15
  12.7 7.7 %delta.1.own_ref = f32[256,128]{1,0:T(8,128)S(1)} custom-call(s32[1]{0:T(128)} %bitcast.side_ref, bf16[16,4,128]{2,1,0:T(4,128)(2,1)S(1)} %copy-done.8, bf16[16,4,128]{2,1,0:T(4,128)(2,1)S(1)} %copy-done.9, bf16[16,8,128]{2,1,0:T(8,128)(2,1)S(1)} %copy-done.6, bf16[16,8,128]{2,1,0:T(8,128)(2,1)S(1)} %copy-done.7, f32[8,16]{1,0:T(8,128)S(1)} %bitcast.12, ...), custom_call_target="tpu_custom_call" | custom-call | tf_op jit(solution)/shard_map/delta/pallas_call | solution.py:146
  20.4 1.5 %collective-permute-start = (f32[256,128]{1,0:T(8,128)S(1)}, f32[256,128]{1,0:T(8,128)S(1)}, u32[]{:S(2)}, u32[]{:S(2)}) collective-permute-start(f32[256,128]{1,0:T(8,128)S(1)} %delta.1.own_ref), channel_id=1, source_target_pairs={{0,64},{64,0},{1,65},{65,1},{2,66},{66,2},{3,67},{67,3},{4,68},{68... | collective-permute-start | bytes 393224 | tf_op jit(solution)/shard_map/ppermute | solution.py:416
  21.9 0.1 reshape.57
  22.0 0.1 gt.17
  22.1 0.0 copy-start.2
  22.1 0.2 convert_reduce_fusion
  22.4 0.1 select_reduce_fusion
  22.5 0.4 collective-permute-done.other_ref
  22.9 1.1 %pack.1 = bf16[6144,128]{1,0:T(8,128)(2,1)S(1)} custom-call(s32[384]{0:T(512)S(1)} %broadcast_subtract_fusion.source_ref, f32[256,128]{1,0:T(8,128)S(1)} %delta.1.own_ref, f32[256,128]{1,0:T(8,128)S(1)} %collective-permute-done.other_ref, f32[16,128]{1,0:T(8,128)S(1)} %bitcast.11), custom_call_target="tpu_custom_call" | custom-call | tf_op jit(solution)/shard_map/pack/pallas_call | solution.py:199
  24.1 34.7 %all_to_all.17.x_ref = bf16[64,96,128]{2,1,0:T(8,128)(2,1)S(1)} all-to-all(bf16[64,96,128]{2,1,0:T(8,128)(2,1)S(1)} %bitcast.10), channel_id=1, replica_groups=mesh['side'=2,'dev'=64] {'dev'}, dimensions={0} | all-to-all | bytes 3145728 | tf_op jit(solution)/shard_map/all_to_all | solution.py:421
  58.8 2.2 %copy-done.3 = bf16[2,2048,512]{2,1,0:T(8,128)(2,1)S(1)} copy-done((bf16[2,2048,512]{2,1,0:T(8,128)(2,1)S(1)}, bf16[2,2048,512]{2,1,0:T(8,128)(2,1)}, u32[]{:S(2)}) %copy-start.3) | copy-done | bytes 4194328
  61.0 2.2 %copy-done.4 = bf16[2,512,2048]{2,1,0:T(8,128)(2,1)S(1)} copy-done((bf16[2,512,2048]{2,1,0:T(8,128)(2,1)S(1)}, bf16[2,512,2048]{2,1,0:T(8,128)(2,1)}, u32[]{:S(2)}) %copy-start.4) | copy-done | bytes 4194328
  63.2 7.6 %experts.1 = bf16[64,96,128]{2,1,0:T(8,128)(2,1)} custom-call(bf16[64,96,128]{2,1,0:T(8,128)(2,1)S(1)} %all_to_all.17.x_ref, bf16[2,2048,512]{2,1,0:T(8,128)(2,1)S(1)} %copy-done.2, bf16[2,2048,512]{2,1,0:T(8,128)(2,1)S(1)} %copy-done.3, bf16[2,512,2048]{2,1,0:T(8,128)(2,1)S(1)} %copy-done.4), custom_call_target="tpu_custom_call" | custom-call | tf_op jit(solution)/shard_map/experts/pallas_call | solution.py:279
  70.8 4.9 %all-to-all-start.1 = ((bf16[64,96,128]{2,1,0:T(8,128)(2,1)}), bf16[64,96,128]{2,1,0:T(8,128)(2,1)S(1)}, u32[]{:S(2)}, u32[]{:S(2)}) async-start(bf16[64,96,128]{2,1,0:T(8,128)(2,1)} %experts.1), calls=%async_computation.1 | async-start | bytes 3145728 | tf_op jit(solution)/shard_map/all_to_all | solution.py:425
  75.7 0.1 reshape.58
  75.8 22.4 %all-to-all-done.1 = bf16[64,96,128]{2,1,0:T(8,128)(2,1)S(1)} async-done(((bf16[64,96,128]{2,1,0:T(8,128)(2,1)}), bf16[64,96,128]{2,1,0:T(8,128)(2,1)S(1)}, u32[]{:S(2)}, u32[]{:S(2)}) %all-to-all-start.1) | async-done | bytes 1572896 | tf_op jit(solution)/shard_map/all_to_all | solution.py:425
  98.2 0.8 combine.1
  99.0 3.0 %collective-permute-start.1 = (f32[128,128]{1,0:T(8,128)S(1)}, f32[128,128]{1,0:T(8,128)S(1)}, u32[]{:S(2)}, u32[]{:S(2)}) collective-permute-start(f32[128,128]{1,0:T(8,128)S(1)} %get-tuple-element.8), channel_id=1, source_target_pairs={{0,64},{64,0},{1,65},{65,1},{2,66},{66,2},{3,67},{67,3},{4,68},{68... | collective-permute-start | bytes 196616 | tf_op jit(solution)/shard_map/ppermute | solution.py:427
  102.1 0.9 collective-permute-done.1.got_ref
  103.0 0.6 last.1
  (26 shorter events, 0.1 us)
Async XLA Ops:
  0.0 3.4 %copy-start = (f32[16,8,128,128]{3,2,1,0:T(8,128)S(1)}, f32[16,8,128,128]{3,2,1,0:T(8,128)}, u32[]{:S(2)}) copy-start(f32[16,8,128,128]{3,2,1,0:T(8,128)} %state_ref.1) | copy-start | bytes 25165828
  3.4 2.2 %copy-start.1 = (bf16[1024,2048]{1,0:T(8,128)(2,1)S(1)}, bf16[1024,2048]{1,0:T(8,128)(2,1)}, u32[]{:S(2)}) copy-start(bf16[1024,2048]{1,0:T(8,128)(2,1)} %weight_hbm.1) | copy-start | bytes 12582916
  5.6 0.8 copy-start.5
  6.4 0.8 copy-start.6
  7.2 0.8 copy-start.7
  7.9 0.7 copy-start.8
  8.6 0.7 copy-start.9
  9.4 0.7 copy-start.11
  10.1 0.7 copy-start.12
  10.7 0.7 copy-start.13
  11.4 0.7 copy-start.14
  12.1 0.7 copy-start.15
  12.7 9.2 %copy-start.16 = (s32[16,10]{1,0:T(8,128)S(1)}, s32[16,10]{1,0:T(8,128)}, u32[]{:S(2)}) copy-start(s32[16,10]{1,0:T(8,128)} %param.31) | copy-start | bytes 1924
  12.7 10.2 %copy-start.10 = (f32[2048]{0:T(1024)S(1)}, f32[2048]{0:T(1024)}, u32[]{:S(2)}) copy-start(f32[2048]{0:T(1024)} %param.30) | copy-start | bytes 24580
  20.4 2.5 %collective-permute-start = (f32[256,128]{1,0:T(8,128)S(1)}, f32[256,128]{1,0:T(8,128)S(1)}, u32[]{:S(2)}, u32[]{:S(2)}) collective-permute-start(f32[256,128]{1,0:T(8,128)S(1)} %delta.1.own_ref), channel_id=1, source_target_pairs={{0,64},{64,0},{1,65},{65,1},{2,66},{66,2},{3,67},{67,3},{4,68},{68... | collective-permute-start | bytes 393224 | tf_op jit(solution)/shard_map/ppermute | solution.py:416
  22.1 36.7 %copy-start.2 = (bf16[2,2048,512]{2,1,0:T(8,128)(2,1)S(1)}, bf16[2,2048,512]{2,1,0:T(8,128)(2,1)}, u32[]{:S(2)}) copy-start(bf16[2,2048,512]{2,1,0:T(8,128)(2,1)} %gate_hbm.1) | copy-start | bytes 12582916
  58.8 2.2 %copy-start.3 = (bf16[2,2048,512]{2,1,0:T(8,128)(2,1)S(1)}, bf16[2,2048,512]{2,1,0:T(8,128)(2,1)}, u32[]{:S(2)}) copy-start(bf16[2,2048,512]{2,1,0:T(8,128)(2,1)} %up_hbm.1) | copy-start | bytes 12582916
  61.0 2.2 %copy-start.4 = (bf16[2,512,2048]{2,1,0:T(8,128)(2,1)S(1)}, bf16[2,512,2048]{2,1,0:T(8,128)(2,1)}, u32[]{:S(2)}) copy-start(bf16[2,512,2048]{2,1,0:T(8,128)(2,1)} %down_hbm.1) | copy-start | bytes 12582916
  63.2 12.6 %copy-start.17 = (f32[16,10]{1,0:T(8,128)S(1)}, f32[16,10]{1,0:T(8,128)}, u32[]{:S(2)}) copy-start(f32[16,10]{1,0:T(8,128)} %param.32) | copy-start | bytes 1924
  70.8 27.4 %all-to-all-start.1 = ((bf16[64,96,128]{2,1,0:T(8,128)(2,1)}), bf16[64,96,128]{2,1,0:T(8,128)(2,1)S(1)}, u32[]{:S(2)}, u32[]{:S(2)}) async-start(bf16[64,96,128]{2,1,0:T(8,128)(2,1)} %experts.1), calls=%async_computation.1 | async-start | bytes 3145728 | tf_op jit(solution)/shard_map/all_to_all | solution.py:425
  99.0 3.9 %collective-permute-start.1 = (f32[128,128]{1,0:T(8,128)S(1)}, f32[128,128]{1,0:T(8,128)S(1)}, u32[]{:S(2)}, u32[]{:S(2)}) collective-permute-start(f32[128,128]{1,0:T(8,128)S(1)} %get-tuple-element.8), channel_id=1, source_target_pairs={{0,64},{64,0},{1,65},{65,1},{2,66},{66,2},{3,67},{67,3},{4,68},{68... | collective-permute-start | bytes 196616 | tf_op jit(solution)/shard_map/ppermute | solution.py:427

commit v2 on v1

--- a/solution.py
+++ b/solution.py
@@ -13,6 +13,10 @@
 MIB = 1 << 20
 
 
+def in_hbm(*arrays):
+    return [pltpu.with_memory_space_constraint(a, pltpu.HBM) for a in arrays]
+
+
 def softplus(x):
     return jnp.maximum(x, 0.0) + jnp.log1p(jnp.exp(-jnp.abs(x)))
 
@@ -32,11 +36,6 @@
         jnp.int32, (n, n), 1
     )
     return jnp.sum(jnp.where(on_diagonal, square, 0.0), axis=1, keepdims=True)
-
-
-def pick_column(table, column):
-    lane = lax.broadcasted_iota(jnp.int32, table.shape, 1)
-    return jnp.sum(jnp.where(lane == column, table, 0.0), axis=1, keepdims=True)
 
 
 def delta_kernel(
@@ -49,128 +48,131 @@
     beta_ref,
     log_ref,
     bias_ref,
-    state_ref,
     gain_ref,
     residual_ref,
+    state_hbm,
     weight_hbm,
     out_ref,
+    state_ref,
     weight_ref,
+    qstate_ref,
+    kstate_ref,
     heads_ref,
+    state_sem,
     weight_sem,
 ):
-    step = pl.program_id(0)
-    steps = pl.num_programs(0)
     tokens, width = residual_ref.shape
     heads = value_ref.shape[1]
     key_heads = query_ref.shape[1]
     repeats = heads // key_heads
     size = query_ref.shape[2]
-    load = pltpu.make_async_copy(weight_hbm, weight_ref, weight_sem)
-
-    @pl.when(step == 0)
-    def _():
+    parts = tokens // STEP_TOKENS
+    loads = [
+        pltpu.make_async_copy(
+            state_hbm.at[pl.ds(i * STEP_TOKENS, STEP_TOKENS)],
+            state_ref.at[pl.ds(i * STEP_TOKENS, STEP_TOKENS)],
+            state_sem.at[i],
+        )
+        for i in range(parts)
+    ]
+    for load in loads:
         load.start()
-
+    weight_load = pltpu.make_async_copy(weight_hbm, weight_ref, weight_sem)
+    weight_load.start()
+
+    def rows(ref):
+        return jnp.concatenate([ref[t].astype(jnp.float32) for t in range(tokens)], 0)
+
+    query_unit = unit_rows(rows(query_ref)) * size ** (-0.5)
+    key_unit = unit_rows(rows(key_ref))
+    count = tokens * key_heads
+    columns = jnp.concatenate([query_unit, key_unit], 0).T
+    products = jnp.broadcast_to(
+        jnp.sum(query_unit * key_unit, -1, keepdims=True), (count, size)
+    )
+    for r in range(repeats):
+        heads_ref[pl.ds(r, count, stride=repeats), :] = products
     retain_all = jnp.exp(
         -jnp.exp(row_to_column(log_ref[...]))
         * softplus(decay_ref[...] + row_to_column(bias_ref[...]))
     )
     rate_all = sigmoid(beta_ref[...])
-    units = []
-    for j in range(STEP_TOKENS):
-        units.append(unit_rows(query_ref[j].astype(jnp.float32)) * size ** (-0.5))
-        units.append(unit_rows(key_ref[j].astype(jnp.float32)))
-    rows = jnp.concatenate(units, 0)
-    columns = rows.T
-    for j in range(STEP_TOKENS):
-        token = step * STEP_TOKENS + j
-        query_unit, key_unit = units[2 * j], units[2 * j + 1]
-        products = jnp.sum(query_unit * key_unit, -1, keepdims=True)
-        qrows, krows, prows = [], [], []
-        for k in range(key_heads):
-            at = 2 * j * key_heads + k
-            qcol = jnp.broadcast_to(columns[:, at : at + 1], (size, size))
-            at = at + key_heads
-            kcol = jnp.broadcast_to(columns[:, at : at + 1], (size, size))
-            for r in range(repeats):
-                state = state_ref[j, k * repeats + r]
-                qrows.append(jnp.sum(qcol * state, axis=0, keepdims=True))
-                krows.append(jnp.sum(kcol * state, axis=0, keepdims=True))
-                prows.append(products[k : k + 1])
-        qstate = jnp.concatenate(qrows, 0)
-        kstate = jnp.concatenate(krows, 0)
-        product = jnp.concatenate(prows, 0)
-        retain = pick_column(retain_all, token)
-        rate = pick_column(rate_all, token)
-        correct = rate * (value_ref[j].astype(jnp.float32) - retain * kstate)
-        attend = retain * qstate + product * correct
-        inv_rms = lax.rsqrt(jnp.mean(attend * attend, -1, keepdims=True) + EPSILON)
-        gate = gate_ref[j].astype(jnp.float32)
-        gated = attend * inv_rms * gain_ref[...] * (gate * sigmoid(gate))
-        heads_ref[pl.ds(pl.multiple_of(token * heads, heads), heads), :] = gated
-
-    @pl.when(step == steps - 1)
-    def _():
-        gated_out = jnp.concatenate(
-            [heads_ref[pl.ds(h, tokens, stride=heads), :] for h in range(heads)], 1
-        ).astype(jnp.bfloat16)
-        load.wait()
-        side = side_ref[0]
-        blocks = width // LANES
-        wide = 4 * LANES
-        for n in range(width // wide):
-            part = jnp.dot(
-                gated_out,
-                weight_ref[:, n * wide : (n + 1) * wide],
-                preferred_element_type=jnp.float32,
-            )
-            kept = residual_ref[:, n * wide : (n + 1) * wide].astype(jnp.float32)
-            part = part + jnp.where(side == 0, kept, 0.0)
-            for f in range(4):
-                out_ref[pl.ds(n * 4 + f, tokens, stride=blocks), :] = part[
-                    :, f * LANES : (f + 1) * LANES
-                ]
+    for i in range(parts):
+        loads[i].wait()
+        for t in range(i * STEP_TOKENS, (i + 1) * STEP_TOKENS):
+            for k in range(key_heads):
+                at = t * key_heads + k
+                qcol = jnp.broadcast_to(columns[:, at : at + 1], (size, size))
+                at = at + count
+                kcol = jnp.broadcast_to(columns[:, at : at + 1], (size, size))
+                for r in range(repeats):
+                    h = k * repeats + r
+                    state = state_ref[t, h]
+                    at = t * heads + h
+                    qstate_ref[at : at + 1, :] = jnp.sum(qcol * state, axis=0, keepdims=True)
+                    kstate_ref[at : at + 1, :] = jnp.sum(kcol * state, axis=0, keepdims=True)
+
+    def per_head(table):
+        return jnp.concatenate(
+            [jnp.broadcast_to(table[:, t : t + 1], (heads, size)) for t in range(tokens)], 0
+        )
+
+    retain, rate = per_head(retain_all), per_head(rate_all)
+    correct = rate * (rows(value_ref) - retain * kstate_ref[...])
+    attend = retain * qstate_ref[...] + heads_ref[...] * correct
+    inv_rms = lax.rsqrt(jnp.mean(attend * attend, -1, keepdims=True) + EPSILON)
+    gate = rows(gate_ref)
+    heads_ref[...] = attend * inv_rms * gain_ref[...] * (gate * sigmoid(gate))
+    gated_out = jnp.concatenate(
+        [heads_ref[pl.ds(h, tokens, stride=heads), :] for h in range(heads)], 1
+    ).astype(jnp.bfloat16)
+    weight_load.wait()
+    side = side_ref[0]
+    blocks = width // LANES
+    wide = 4 * LANES
+    for n in range(width // wide):
+        part = jnp.dot(
+            gated_out,
+            weight_ref[:, n * wide : (n + 1) * wide],
+            preferred_element_type=jnp.float32,
+        )
+        kept = residual_ref[:, n * wide : (n + 1) * wide].astype(jnp.float32)
+        part = part + jnp.where(side == 0, kept, 0.0)
+        for f in range(4):
+            out_ref[pl.ds(n * 4 + f, tokens, stride=blocks), :] = part[
+                :, f * LANES : (f + 1) * LANES
+            ]
 
 
 def delta_call(side, query, key_in, value, gate, decay, beta, log, bias, states, gain, residual, weight):
     tokens, heads, size = value.shape
-    key_heads = query.shape[1]
     width = residual.shape[1]
-
-    def by_token(*shape):
-        return pl.BlockSpec((STEP_TOKENS,) + shape, lambda i: (i,) + (0,) * len(shape))
+    small = (query, key_in, value, gate, decay, beta, log, bias, gain, residual)
 
     def whole(array):
         return pl.BlockSpec(array.shape, lambda i: (0,) * array.ndim)
 
+    pairs = pltpu.VMEM((tokens * heads, size), jnp.float32)
     return pl.pallas_call(
         delta_kernel,
-        grid=(tokens // STEP_TOKENS,),
+        grid=(1,),
         out_shape=jax.ShapeDtypeStruct((tokens * width // LANES, LANES), jnp.float32),
-        in_specs=[
-            pl.BlockSpec(memory_space=pltpu.SMEM),
-            by_token(key_heads, size),
-            by_token(key_heads, size),
-            by_token(heads, size),
-            by_token(heads, size),
-            whole(decay),
-            whole(beta),
-            whole(log),
-            whole(bias),
-            by_token(heads, size, size),
-            whole(gain),
-            whole(residual),
-            pl.BlockSpec(memory_space=pl.ANY),
-        ],
+        in_specs=[pl.BlockSpec(memory_space=pltpu.SMEM)]
+        + [whole(a) for a in small]
+        + [pl.BlockSpec(memory_space=pl.ANY)] * 2,
         out_specs=pl.BlockSpec((tokens * width // LANES, LANES), lambda i: (0, 0)),
         scratch_shapes=[
+            pltpu.VMEM(states.shape, states.dtype),
             pltpu.VMEM(weight.shape, weight.dtype),
-            pltpu.VMEM((tokens * heads, size), jnp.float32),
+            pairs,
+            pairs,
+            pairs,
+            pltpu.SemaphoreType.DMA((tokens // STEP_TOKENS,)),
             pltpu.SemaphoreType.DMA,
         ],
-        compiler_params=pltpu.CompilerParams(vmem_limit_bytes=16 * MIB),
+        compiler_params=pltpu.CompilerParams(vmem_limit_bytes=24 * MIB),
         name="delta",
-    )(side, query, key_in, value, gate, decay, beta, log, bias, states, gain, residual, weight)
+    )(side, *in_hbm(*small, states, weight))
 
 
 def pack_kernel(source_ref, own_ref, other_ref, gain_ref, out_ref, tiles_ref):
@@ -290,7 +292,7 @@
         ],
         compiler_params=pltpu.CompilerParams(vmem_limit_bytes=32 * MIB),
         name="experts",
-    )(received, w_gate, w_up, w_down)
+    )(received, *in_hbm(w_gate, w_up, w_down))
 
 
 def gather_kernel(side_ref, slot_ref, weight_ref, back_ref, keep_ref, send_ref, sums_ref):
@@ -364,11 +366,26 @@
     position = jnp.sum(same.astype(jnp.int32), axis=1)
     local = ids - side_index * per_side
     on_side = (local >= 0) & (local < per_side)
-    slot = jnp.where(on_side, local * CAP + position, -1)
+    dev = local // experts
+    place = jnp.where(side_index == 0, dev, per_side // experts - 1 - dev)
+    slot = jnp.where(on_side, (place * experts + local % experts) * CAP + position, -1)
     weights = jnp.where(on_side, route_weight.reshape(-1), 0.0)
     hit = slot[None, :] == lax.broadcasted_iota(jnp.int32, (per_side * CAP, entries), 0)
     source = tokens - jnp.sum(jnp.where(hit, tokens - token[None, :], 0), axis=1)
     return source, jnp.maximum(slot, 0), weights
+
+
+def exchange(rows, dev_count):
+    ahead = list(range(dev_count))
+    groups = [ahead, [dev_count + d for d in reversed(ahead)]]
+    return lax.all_to_all(
+        rows,
+        ("side", "dev"),
+        split_axis=0,
+        concat_axis=0,
+        axis_index_groups=groups,
+        tiled=True,
+    )
 
 
 def body(
@@ -418,11 +435,11 @@
         route_ids, route_weight, side_index, dev_count * experts, experts
     )
     send_rows = pack_call(source, own, other, post_gain.reshape(blocks, LANES))
-    received = lax.all_to_all(send_rows, "dev", split_axis=0, concat_axis=0, tiled=True)
+    received = exchange(send_rows, dev_count)
     expert_out = expert_call(
         received.reshape(dev_count, -1, LANES), w_gate, w_up, w_down
     ).reshape(received.shape)
-    back = lax.all_to_all(expert_out, "dev", split_axis=0, concat_axis=0, tiled=True)
+    back = exchange(expert_out, dev_count)
     keep, send = gather_call(side, slots, weights, back, tokens, blocks)
     got = lax.ppermute(send, "side", swap)
     return last_call(side, own, other, keep, got, tokens)

time: 104 us -> 82.5 us (0.79)
  local copies, waits for them, and re-layouts: 17.3 us -> 0.27 us
  starting transfers between devices: 9.46 us -> 14.6 us
  waiting for transfers between devices: 23.7 us -> 18.7 us
  blocking collectives: 34.7 us -> 30.9 us
    unnamed x36 -> x6, local copies, waits for them, and re-layouts: 17.1 us -> 0.01 us
    all_to_all x1, starting transfers between devices: 4.93 us -> 10.1 us  [exchange(): lax.all_to_all(rows, ('side', 'dev'), split_axis=0, concat_axis=0, axis_i...]
    all_to_all x1, waiting for transfers between devices: 22.4 us -> 17.4 us  [exchange(): lax.all_to_all(rows, ('side', 'dev'), split_axis=0, concat_axis=0, axis_i...]
    all_to_all x1, blocking collectives: 34.7 us -> 30.9 us  [exchange(): lax.all_to_all(rows, ('side', 'dev'), split_axis=0, concat_axis=0, axis_i...]
    pallas_call x1, Pallas kernels: 7.72 us -> 6.41 us  [delta_call(): pl.pallas_call(delta_kernel, grid=(1,), out_shape=jax.ShapeDtypeStruct((t...]
where the time goes in v2:
time: 82.5 us; the launch traced here: 82.2 us
  blocking collectives  30.9 us (37%)
  waiting for transfers between devices  18.7 us (23%)
  Pallas kernels  17.3 us (21%)
  starting transfers between devices  14.6 us (18%)
    all_to_all x1, blocking collectives, exchange(): lax.all_to_all(rows, ('side', 'dev'), split_axis=0, concat_axis=0, axis_i...  30.9 us
    all_to_all x1, waiting for transfers between devices, exchange(): lax.all_to_all(rows, ('side', 'dev'), split_axis=0, concat_axis=0, axis_i...  17.4 us
    all_to_all x1, starting transfers between devices, exchange(): lax.all_to_all(rows, ('side', 'dev'), split_axis=0, concat_axis=0, axis_i...  10.1 us
    pallas_call x1, Pallas kernels, expert_call(): pl.pallas_call(expert_kernel, out_shape=jax.ShapeDtypeStruct(received.sha...  8.22 us
    pallas_call x1, Pallas kernels, delta_call(): pl.pallas_call(delta_kernel, grid=(1,), out_shape=jax.ShapeDtypeStruct((t...  6.41 us
    ppermute x1, starting transfers between devices, body(): got = lax.ppermute(send, 'side', swap)  3.03 us
  transfers between devices with their start and end apart: 3, of which 3 were waited for; matrix products, arithmetic and copies ran while one was open for 1% of the time, Pallas kernels for 0%

profile of v2, /device:TPU:1, one launch (start us, length us, event | category | flops | bytes accessed | tf_op | source)
XLA Modules:
  0.0 82.2 jit_solution(2515049135161915779)
XLA Ops:
  0.0 0.0 copy-start.1
  0.0 0.0 copy-start
  0.0 6.4 %delta.1.own_ref = f32[256,128]{1,0:T(8,128)S(1)} custom-call(s32[1]{0:T(128)} %bitcast.side_ref, bf16[16,4,128]{2,1,0:T(4,128)(2,1)} %query_ref.1, bf16[16,4,128]{2,1,0:T(4,128)(2,1)} %key_ref.1, bf16[16,8,128]{2,1,0:T(8,128)(2,1)} %value_ref.1, bf16[16,8,128]{2,1,0:T(8,128)(2,1)} %gate_ref.1, f32[8,16]{1,0:T(8,128)} %bitcast.12, f32[8,16]{1,0:T(8,128)} %bitcast.13, ...), custom_call_target="tpu_custom_call" | custom-call | tf_op jit(solution)/shard_map/delta/pallas_call | solution.py:156
  6.4 1.5 %collective-permute-start = (f32[256,128]{1,0:T(8,128)S(1)}, f32[256,128]{1,0:T(8,128)S(1)}, u32[]{:S(2)}, u32[]{:S(2)}) collective-permute-start(f32[256,128]{1,0:T(8,128)S(1)} %delta.1.own_ref), channel_id=1, source_target_pairs={{0,64},{64,0},{1,65},{65,1},{2,66},{66,2},{3,67},{67,3},{4,68},{68... | collective-permute-start | bytes 393224 | tf_op jit(solution)/shard_map/ppermute | solution.py:433
  7.9 0.0 copy-done.1
  7.9 0.1 reshape.87
  8.0 0.1 gt.17
  8.1 0.2 convert_reduce_fusion
  8.4 0.1 select_reduce_fusion
  8.5 0.4 collective-permute-done.other_ref
  8.9 0.0 copy-done
  8.9 1.1 %pack.1 = bf16[6144,128]{1,0:T(8,128)(2,1)S(1)} custom-call(s32[384]{0:T(512)S(1)} %broadcast_subtract_fusion.source_ref, f32[256,128]{1,0:T(8,128)S(1)} %delta.1.own_ref, f32[256,128]{1,0:T(8,128)S(1)} %collective-permute-done.other_ref, f32[16,128]{1,0:T(8,128)S(1)} %bitcast.11), custom_call_target="tpu_custom_call" | custom-call | tf_op jit(solution)/shard_map/pack/pallas_call | solution.py:201
  10.1 30.9 %all_to_all.17.x_ref = bf16[64,96,128]{2,1,0:T(8,128)(2,1)S(1)} all-to-all(bf16[64,96,128]{2,1,0:T(8,128)(2,1)S(1)} %bitcast.10), channel_id=1, replica_groups={{0,1,2,3,4,5,6,7,8,9,10,11,12,13,14,15,16,17,18,19,20,21,22,23,24,25,26..., dimensions={0} | all-to-all | bytes 3145728 | tf_op jit(solution)/shard_map/all_to_all | solution.py:381
  40.9 0.0 copy-start.2
  40.9 8.2 %experts.1 = bf16[64,96,128]{2,1,0:T(8,128)(2,1)} custom-call(bf16[64,96,128]{2,1,0:T(8,128)(2,1)S(1)} %all_to_all.17.x_ref, bf16[2,2048,512]{2,1,0:T(8,128)(2,1)} %gate_hbm.1, bf16[2,2048,512]{2,1,0:T(8,128)(2,1)} %up_hbm.1, bf16[2,512,2048]{2,1,0:T(8,128)(2,1)} %down_hbm.1), custom_call_target="tpu_custom_call" | custom-call | tf_op jit(solution)/shard_map/experts/pallas_call | solution.py:281
  49.2 10.1 %all-to-all-start.1 = ((bf16[64,96,128]{2,1,0:T(8,128)(2,1)}), bf16[64,96,128]{2,1,0:T(8,128)(2,1)S(1)}, u32[]{:S(2)}, u32[]{:S(2)}) async-start(bf16[64,96,128]{2,1,0:T(8,128)(2,1)} %experts.1), calls=%async_computation.1 | async-start | bytes 3145728 | tf_op jit(solution)/shard_map/all_to_all | solution.py:381
  59.3 0.0 copy-done.2
  59.3 0.1 reshape.88
  59.4 17.4 %all-to-all-done.1 = bf16[64,96,128]{2,1,0:T(8,128)(2,1)S(1)} async-done(((bf16[64,96,128]{2,1,0:T(8,128)(2,1)}), bf16[64,96,128]{2,1,0:T(8,128)(2,1)S(1)}, u32[]{:S(2)}, u32[]{:S(2)}) %all-to-all-start.1) | async-done | bytes 1572896 | tf_op jit(solution)/shard_map/all_to_all | solution.py:381
  76.8 0.8 %combine.1 = (f32[128,128]{1,0:T(8,128)S(1)}, f32[128,128]{1,0:T(8,128)S(1)}) custom-call(s32[1]{0:T(128)} %bitcast.side_ref, s32[160]{0:T(256)S(1)} %get-tuple-element.9.slot_ref, f32[160]{0:T(256)S(1)} %broadcast_select_fusion.weight_ref, bf16[6144,128]{1,0:T(8,128)(2,1)S(1)} %bitcast.9), custom_call_target="tpu_custom_call" | custom-call | tf_op jit(solution)/shard_map/combine/pallas_call | solution.py:321
  77.7 3.0 %collective-permute-start.1 = (f32[128,128]{1,0:T(8,128)S(1)}, f32[128,128]{1,0:T(8,128)S(1)}, u32[]{:S(2)}, u32[]{:S(2)}) collective-permute-start(f32[128,128]{1,0:T(8,128)S(1)} %get-tuple-element.8), channel_id=1, source_target_pairs={{0,64},{64,0},{1,65},{65,1},{2,66},{66,2},{3,67},{67,3},{4,68},{68... | collective-permute-start | bytes 196616 | tf_op jit(solution)/shard_map/ppermute | solution.py:444
  80.7 0.9 %collective-permute-done.1.got_ref = f32[128,128]{1,0:T(8,128)S(1)} collective-permute-done((f32[128,128]{1,0:T(8,128)S(1)}, f32[128,128]{1,0:T(8,128)S(1)}, u32[]{:S(2)}, u32[]{:S(2)}) %collective-permute-start.1) | collective-permute-done | bytes 65568 | tf_op jit(solution)/shard_map/ppermute | solution.py:444
  81.6 0.6 last.1
  (5 shorter events, 0.0 us)
Async XLA Ops:
  0.0 7.9 %copy-start.1 = (s32[16,10]{1,0:T(8,128)S(1)}, s32[16,10]{1,0:T(8,128)}, u32[]{:S(2)}) copy-start(s32[16,10]{1,0:T(8,128)} %param.31) | copy-start | bytes 1924
  0.0 8.9 %copy-start = (f32[2048]{0:T(1024)S(1)}, f32[2048]{0:T(1024)}, u32[]{:S(2)}) copy-start(f32[2048]{0:T(1024)} %param.30) | copy-start | bytes 24580
  6.4 2.5 %collective-permute-start = (f32[256,128]{1,0:T(8,128)S(1)}, f32[256,128]{1,0:T(8,128)S(1)}, u32[]{:S(2)}, u32[]{:S(2)}) collective-permute-start(f32[256,128]{1,0:T(8,128)S(1)} %delta.1.own_ref), channel_id=1, source_target_pairs={{0,64},{64,0},{1,65},{65,1},{2,66},{66,2},{3,67},{67,3},{4,68},{68... | collective-permute-start | bytes 393224 | tf_op jit(solution)/shard_map/ppermute | solution.py:433
  40.9 18.3 %copy-start.2 = (f32[16,10]{1,0:T(8,128)S(1)}, f32[16,10]{1,0:T(8,128)}, u32[]{:S(2)}) copy-start(f32[16,10]{1,0:T(8,128)} %param.32) | copy-start | bytes 1924
  49.2 27.6 %all-to-all-start.1 = ((bf16[64,96,128]{2,1,0:T(8,128)(2,1)}), bf16[64,96,128]{2,1,0:T(8,128)(2,1)S(1)}, u32[]{:S(2)}, u32[]{:S(2)}) async-start(bf16[64,96,128]{2,1,0:T(8,128)(2,1)} %experts.1), calls=%async_computation.1 | async-start | bytes 3145728 | tf_op jit(solution)/shard_map/all_to_all | solution.py:381
  77.7 3.9 %collective-permute-start.1 = (f32[128,128]{1,0:T(8,128)S(1)}, f32[128,128]{1,0:T(8,128)S(1)}, u32[]{:S(2)}, u32[]{:S(2)}) collective-permute-start(f32[128,128]{1,0:T(8,128)S(1)} %get-tuple-element.8), channel_id=1, source_target_pairs={{0,64},{64,0},{1,65},{65,1},{2,66},{66,2},{3,67},{67,3},{4,68},{68... | collective-permute-start | bytes 196616 | tf_op jit(solution)/shard_map/ppermute | solution.py:444

commit v3 on v2

--- a/solution.py
+++ b/solution.py
@@ -38,35 +38,22 @@
     return jnp.sum(jnp.where(on_diagonal, square, 0.0), axis=1, keepdims=True)
 
 
-def delta_kernel(
-    side_ref,
-    query_ref,
-    key_ref,
-    value_ref,
-    gate_ref,
-    decay_ref,
-    beta_ref,
-    log_ref,
-    bias_ref,
-    gain_ref,
-    residual_ref,
-    state_hbm,
-    weight_hbm,
-    out_ref,
-    state_ref,
-    weight_ref,
-    qstate_ref,
-    kstate_ref,
-    heads_ref,
-    state_sem,
-    weight_sem,
-):
+def delta_kernel(side_ref, *refs):
+    small_hbm, state_hbm, weight_hbm, out_ref = refs[:10], refs[10], refs[11], refs[12]
+    small_refs, refs = refs[13:23], refs[23:]
+    state_ref, weight_ref, qstate_ref, kstate_ref, heads_ref, small_sem, state_sem, weight_sem = refs
+    query_ref, key_ref, value_ref, gate_ref, decay_ref = small_refs[:5]
+    beta_ref, log_ref, bias_ref, gain_ref, residual_ref = small_refs[5:]
     tokens, width = residual_ref.shape
     heads = value_ref.shape[1]
     key_heads = query_ref.shape[1]
     repeats = heads // key_heads
     size = query_ref.shape[2]
     parts = tokens // STEP_TOKENS
+    smalls = [
+        pltpu.make_async_copy(source, target, small_sem.at[i])
+        for i, (source, target) in enumerate(zip(small_hbm, small_refs))
+    ]
     loads = [
         pltpu.make_async_copy(
             state_hbm.at[pl.ds(i * STEP_TOKENS, STEP_TOKENS)],
@@ -75,10 +62,11 @@
         )
         for i in range(parts)
     ]
-    for load in loads:
+    weight_load = pltpu.make_async_copy(weight_hbm, weight_ref, weight_sem)
+    for load in smalls[:2] + loads[:2] + smalls[2:] + loads[2:] + [weight_load]:
         load.start()
-    weight_load = pltpu.make_async_copy(weight_hbm, weight_ref, weight_sem)
-    weight_load.start()
+    for load in smalls[:2]:
+        load.wait()
 
     def rows(ref):
         return jnp.concatenate([ref[t].astype(jnp.float32) for t in range(tokens)], 0)
@@ -92,11 +80,6 @@
     )
     for r in range(repeats):
         heads_ref[pl.ds(r, count, stride=repeats), :] = products
-    retain_all = jnp.exp(
-        -jnp.exp(row_to_column(log_ref[...]))
-        * softplus(decay_ref[...] + row_to_column(bias_ref[...]))
-    )
-    rate_all = sigmoid(beta_ref[...])
     for i in range(parts):
         loads[i].wait()
         for t in range(i * STEP_TOKENS, (i + 1) * STEP_TOKENS):
@@ -111,6 +94,14 @@
                     at = t * heads + h
                     qstate_ref[at : at + 1, :] = jnp.sum(qcol * state, axis=0, keepdims=True)
                     kstate_ref[at : at + 1, :] = jnp.sum(kcol * state, axis=0, keepdims=True)
+
+    for load in smalls[2:]:
+        load.wait()
+    retain_all = jnp.exp(
+        -jnp.exp(row_to_column(log_ref[...]))
+        * softplus(decay_ref[...] + row_to_column(bias_ref[...]))
+    )
+    rate_all = sigmoid(beta_ref[...])
 
     def per_head(table):
         return jnp.concatenate(
@@ -148,25 +139,22 @@
     tokens, heads, size = value.shape
     width = residual.shape[1]
     small = (query, key_in, value, gate, decay, beta, log, bias, gain, residual)
-
-    def whole(array):
-        return pl.BlockSpec(array.shape, lambda i: (0,) * array.ndim)
-
+    vmem = pl.BlockSpec(memory_space=pltpu.VMEM)
     pairs = pltpu.VMEM((tokens * heads, size), jnp.float32)
     return pl.pallas_call(
         delta_kernel,
-        grid=(1,),
         out_shape=jax.ShapeDtypeStruct((tokens * width // LANES, LANES), jnp.float32),
         in_specs=[pl.BlockSpec(memory_space=pltpu.SMEM)]
-        + [whole(a) for a in small]
-        + [pl.BlockSpec(memory_space=pl.ANY)] * 2,
-        out_specs=pl.BlockSpec((tokens * width // LANES, LANES), lambda i: (0, 0)),
-        scratch_shapes=[
+        + [pl.BlockSpec(memory_space=pl.ANY)] * (len(small) + 2),
+        out_specs=vmem,
+        scratch_shapes=[pltpu.VMEM(a.shape, a.dtype) for a in small]
+        + [
             pltpu.VMEM(states.shape, states.dtype),
             pltpu.VMEM(weight.shape, weight.dtype),
             pairs,
             pairs,
             pairs,
+            pltpu.SemaphoreType.DMA((len(small),)),
             pltpu.SemaphoreType.DMA((tokens // STEP_TOKENS,)),
             pltpu.SemaphoreType.DMA,
         ],
@@ -209,46 +197,55 @@
     )(source, own, other, gain)
 
 
-def expert_kernel(
-    x_ref, gate_hbm, up_hbm, down_hbm, out_ref, gate_ref, up_ref, down_ref, rows_ref, sems
-):
-    experts, width, units = gate_hbm.shape
+def expert_kernel(x_ref, gate_ref, up_hbm, down_hbm, out_ref, up_ref, down_ref, rows_ref, sems):
+    experts, width, units = gate_ref.shape
     sources = x_ref.shape[0]
     blocks = width // LANES
     groups = sources // TILE
+    count = groups * CAP * TILE
+    wide = 4 * LANES
     copies = []
     for e in range(experts):
-        for i, (hbm, ref) in enumerate(
-            ((gate_hbm, gate_ref), (up_hbm, up_ref), (down_hbm, down_ref))
-        ):
-            copies.append(pltpu.make_async_copy(hbm.at[e], ref.at[e], sems.at[e, i]))
-            copies[-1].start()
+        copies.append(pltpu.make_async_copy(up_hbm.at[e], up_ref.at[e], sems.at[2 * e]))
+        copies.append(pltpu.make_async_copy(down_hbm.at[e], down_ref.at[e], sems.at[2 * e + 1]))
+    for copy in copies[:2]:
+        copy.start()
     row = lax.broadcasted_iota(jnp.int32, (TILE * blocks, TILE * blocks), 0)
     column = lax.broadcasted_iota(jnp.int32, (TILE * blocks, TILE * blocks), 1)
     swap = jnp.where((row % TILE) * TILE + row // TILE == column, 1.0, 0.0).astype(jnp.bfloat16)
+    places = [(g, c) for g in range(groups) for c in range(CAP)]
+
+    def turn(pair):
+        turned = jnp.dot(swap, jnp.concatenate(pair, 1), preferred_element_type=jnp.float32)
+        turned = turned.astype(jnp.bfloat16)
+        return turned[:, :LANES], turned[:, LANES:]
+
+    def place_of(e, g, c):
+        return g * TILE, (e * CAP + c) * blocks
+
     for e in range(experts):
-        for g in range(groups):
-            for c in range(CAP):
-                at = (e * CAP + c) * blocks
-                block = x_ref[g * TILE : (g + 1) * TILE, at : at + blocks, :]
-                block = block.reshape(TILE * blocks, LANES)
-                turned = jnp.dot(swap, block, preferred_element_type=jnp.float32)
-                turned = turned.astype(jnp.bfloat16)
-                r = ((e * groups + g) * CAP + c) * TILE
+        for n in range(0, len(places), 2):
+            pair = []
+            for g, c in places[n : n + 2]:
+                top, at = place_of(e, g, c)
+                block = x_ref[top : top + TILE, at : at + blocks, :]
+                pair.append(block.reshape(TILE * blocks, LANES))
+            for i, turned in enumerate(turn(pair)):
+                r = e * count + (n + i) * TILE
                 for f in range(blocks):
                     rows_ref[r : r + TILE, f * LANES : (f + 1) * LANES] = turned[
                         f * TILE : (f + 1) * TILE
                     ]
-    count = groups * CAP * TILE
-    for e in range(experts):
         x = rows_ref[e * count : (e + 1) * count, :]
-        copies[3 * e].wait()
         gate = jnp.dot(x, gate_ref[e], preferred_element_type=jnp.float32)
-        copies[3 * e + 1].wait()
+        copies[2 * e].wait()
+        if e + 1 < experts:
+            copies[2 * e + 2].start()
         up = jnp.dot(x, up_ref[e], preferred_element_type=jnp.float32)
         inner = (gate * sigmoid(gate) * up).astype(jnp.bfloat16)
-        copies[3 * e + 2].wait()
-        wide = 4 * LANES
+        copies[2 * e + 1].wait()
+        if e + 1 < experts:
+            copies[2 * e + 3].start()
         for n in range(width // wide):
             y = jnp.dot(
                 inner, down_ref[e, :, n * wide : (n + 1) * wide], preferred_element_type=jnp.float32
@@ -256,21 +253,24 @@
             rows_ref[e * count : (e + 1) * count, n * wide : (n + 1) * wide] = y.astype(
                 jnp.bfloat16
             )
-        for g in range(groups):
-            for c in range(CAP):
-                r = ((e * groups + g) * CAP + c) * TILE
-                block = jnp.concatenate(
-                    [
-                        rows_ref[r : r + TILE, f * LANES : (f + 1) * LANES]
-                        for f in range(blocks)
-                    ],
-                    0,
+        for n in range(0, len(places), 2):
+            pair = []
+            for i in range(2):
+                r = e * count + (n + i) * TILE
+                pair.append(
+                    jnp.concatenate(
+                        [
+                            rows_ref[r : r + TILE, f * LANES : (f + 1) * LANES]
+                            for f in range(blocks)
+                        ],
+                        0,
+                    )
                 )
-                turned = jnp.dot(swap, block, preferred_element_type=jnp.float32)
-                at = (e * CAP + c) * blocks
-                out_ref[g * TILE : (g + 1) * TILE, at : at + blocks, :] = turned.astype(
-                    jnp.bfloat16
-                ).reshape(TILE, blocks, LANES)
+            for (g, c), turned in zip(places[n : n + 2], turn(pair)):
+                top, at = place_of(e, g, c)
+                out_ref[top : top + TILE, at : at + blocks, :] = turned.reshape(
+                    TILE, blocks, LANES
+                )
 
 
 def expert_call(received, w_gate, w_up, w_down):
@@ -281,18 +281,17 @@
     return pl.pallas_call(
         expert_kernel,
         out_shape=jax.ShapeDtypeStruct(received.shape, received.dtype),
-        in_specs=[vmem, hbm, hbm, hbm],
+        in_specs=[vmem, vmem, hbm, hbm],
         out_specs=vmem,
         scratch_shapes=[
-            pltpu.VMEM(w_gate.shape, w_gate.dtype),
             pltpu.VMEM(w_up.shape, w_up.dtype),
             pltpu.VMEM(w_down.shape, w_down.dtype),
             pltpu.VMEM((slots, width), jnp.bfloat16),
-            pltpu.SemaphoreType.DMA((experts, 3)),
+            pltpu.SemaphoreType.DMA((2 * experts,)),
         ],
-        compiler_params=pltpu.CompilerParams(vmem_limit_bytes=32 * MIB),
+        compiler_params=pltpu.CompilerParams(vmem_limit_bytes=24 * MIB),
         name="experts",
-    )(received, *in_hbm(w_gate, w_up, w_down))
+    )(received, w_gate, *in_hbm(w_up, w_down))
 
 
 def gather_kernel(side_ref, slot_ref, weight_ref, back_ref, keep_ref, send_ref, sums_ref):

time: 82.5 us -> 80.2 us (0.972)
  Pallas kernels: 17.3 us -> 15 us
    pallas_call x1, Pallas kernels: 8.22 us -> 6.73 us  [expert_call(): pl.pallas_call(expert_kernel, out_shape=jax.ShapeDtypeStruct(received.sha...]
where the time goes in v3:
time: 80.2 us; the launch traced here: 79.9 us
  blocking collectives  30.9 us (39%)
  waiting for transfers between devices  18.7 us (23%)
  Pallas kernels  15 us (19%)
  starting transfers between devices  14.6 us (18%)
    all_to_all x1, blocking collectives, exchange(): lax.all_to_all(rows, ('side', 'dev'), split_axis=0, concat_axis=0, axis_i...  30.9 us
    all_to_all x1, waiting for transfers between devices, exchange(): lax.all_to_all(rows, ('side', 'dev'), split_axis=0, concat_axis=0, axis_i...  17.4 us
    all_to_all x1, starting transfers between devices, exchange(): lax.all_to_all(rows, ('side', 'dev'), split_axis=0, concat_axis=0, axis_i...  10.1 us
    pallas_call x1, Pallas kernels, expert_call(): pl.pallas_call(expert_kernel, out_shape=jax.ShapeDtypeStruct(received.sha...  6.73 us
    pallas_call x1, Pallas kernels, delta_call(): pl.pallas_call(delta_kernel, out_shape=jax.ShapeDtypeStruct((tokens * wid...  5.62 us
    ppermute x1, starting transfers between devices, body(): got = lax.ppermute(send, 'side', swap)  3.05 us
  transfers between devices with their start and end apart: 3, of which 3 were waited for; matrix products, arithmetic and copies ran while one was open for 1% of the time, Pallas kernels for 0%

profile of v3, /device:TPU:1, one launch (start us, length us, event | category | flops | bytes accessed | tf_op | source)
XLA Modules:
  0.0 79.9 jit_solution(2752355451970082225)
XLA Ops:
  0.0 0.0 copy-start.2
  0.0 0.0 copy-start.1
  0.0 5.6 %delta.1.own_ref = f32[256,128]{1,0:T(8,128)S(1)} custom-call(s32[1]{0:T(128)} %bitcast.side_ref, bf16[16,4,128]{2,1,0:T(4,128)(2,1)} %refs_0_.1, bf16[16,4,128]{2,1,0:T(4,128)(2,1)} %refs_1_.1, bf16[16,8,128]{2,1,0:T(8,128)(2,1)} %refs_2_.1, bf16[16,8,128]{2,1,0:T(8,128)(2,1)} %refs_3_.1, f32[8,16]{1,0:T(8,128)} %bitcast.12, f32[8,16]{1,0:T(8,128)} %bitcast.13, ...), custom_call_target="tpu_custom_call" | custom-call | tf_op jit(solution)/shard_map/delta/pallas_call | solution.py:144
  5.6 1.5 %collective-permute-start = (f32[256,128]{1,0:T(8,128)S(1)}, f32[256,128]{1,0:T(8,128)S(1)}, u32[]{:S(2)}, u32[]{:S(2)}) collective-permute-start(f32[256,128]{1,0:T(8,128)S(1)} %delta.1.own_ref), channel_id=1, source_target_pairs={{0,64},{64,0},{1,65},{65,1},{2,66},{66,2},{3,67},{67,3},{4,68},{68... | collective-permute-start | bytes 393224 | tf_op jit(solution)/shard_map/ppermute | solution.py:432
  7.1 0.0 copy-done.2
  7.1 0.1 reshape.87
  7.2 0.1 gt.17
  7.3 0.0 copy-start
  7.3 0.2 convert_reduce_fusion
  7.6 0.1 select_reduce_fusion
  7.7 0.4 collective-permute-done.other_ref
  8.1 0.0 copy-done.1
  8.1 1.1 %pack.1 = bf16[6144,128]{1,0:T(8,128)(2,1)S(1)} custom-call(s32[384]{0:T(512)S(1)} %broadcast_subtract_fusion.source_ref, f32[256,128]{1,0:T(8,128)S(1)} %delta.1.own_ref, f32[256,128]{1,0:T(8,128)S(1)} %collective-permute-done.other_ref, f32[16,128]{1,0:T(8,128)S(1)} %bitcast.11), custom_call_target="tpu_custom_call" | custom-call | tf_op jit(solution)/shard_map/pack/pallas_call | solution.py:189
  9.3 30.9 %all_to_all.17.x_ref = bf16[64,96,128]{2,1,0:T(8,128)(2,1)S(1)} all-to-all(bf16[64,96,128]{2,1,0:T(8,128)(2,1)S(1)} %bitcast.10), channel_id=1, replica_groups={{0,1,2,3,4,5,6,7,8,9,10,11,12,13,14,15,16,17,18,19,20,21,22,23,24,25,26..., dimensions={0} | all-to-all | bytes 3145728 | tf_op jit(solution)/shard_map/all_to_all | solution.py:380
  40.2 0.0 copy-done
  40.2 0.0 copy-start.3
  40.2 6.7 %experts.1 = bf16[64,96,128]{2,1,0:T(8,128)(2,1)} custom-call(bf16[64,96,128]{2,1,0:T(8,128)(2,1)S(1)} %all_to_all.17.x_ref, bf16[2,2048,512]{2,1,0:T(8,128)(2,1)S(1)} %copy-done, bf16[2,2048,512]{2,1,0:T(8,128)(2,1)} %up_hbm.1, bf16[2,512,2048]{2,1,0:T(8,128)(2,1)} %down_hbm.1), custom_call_target="tpu_custom_call" | custom-call | tf_op jit(solution)/shard_map/experts/pallas_call | solution.py:281
  46.9 10.1 %all-to-all-start.1 = ((bf16[64,96,128]{2,1,0:T(8,128)(2,1)}), bf16[64,96,128]{2,1,0:T(8,128)(2,1)S(1)}, u32[]{:S(2)}, u32[]{:S(2)}) async-start(bf16[64,96,128]{2,1,0:T(8,128)(2,1)} %experts.1), calls=%async_computation.1 | async-start | bytes 3145728 | tf_op jit(solution)/shard_map/all_to_all | solution.py:380
  57.0 0.0 copy-done.3
  57.0 0.1 reshape.88
  57.1 17.4 %all-to-all-done.1 = bf16[64,96,128]{2,1,0:T(8,128)(2,1)S(1)} async-done(((bf16[64,96,128]{2,1,0:T(8,128)(2,1)}), bf16[64,96,128]{2,1,0:T(8,128)(2,1)S(1)}, u32[]{:S(2)}, u32[]{:S(2)}) %all-to-all-start.1) | async-done | bytes 1572896 | tf_op jit(solution)/shard_map/all_to_all | solution.py:380
  74.5 0.8 %combine.1 = (f32[128,128]{1,0:T(8,128)S(1)}, f32[128,128]{1,0:T(8,128)S(1)}) custom-call(s32[1]{0:T(128)} %bitcast.side_ref, s32[160]{0:T(256)S(1)} %get-tuple-element.9.slot_ref, f32[160]{0:T(256)S(1)} %broadcast_select_fusion.weight_ref, bf16[6144,128]{1,0:T(8,128)(2,1)S(1)} %bitcast.9), custom_call_target="tpu_custom_call" | custom-call | tf_op jit(solution)/shard_map/combine/pallas_call | solution.py:320
  75.3 3.0 %collective-permute-start.1 = (f32[128,128]{1,0:T(8,128)S(1)}, f32[128,128]{1,0:T(8,128)S(1)}, u32[]{:S(2)}, u32[]{:S(2)}) collective-permute-start(f32[128,128]{1,0:T(8,128)S(1)} %get-tuple-element.8), channel_id=1, source_target_pairs={{0,64},{64,0},{1,65},{65,1},{2,66},{66,2},{3,67},{67,3},{4,68},{68... | collective-permute-start | bytes 196616 | tf_op jit(solution)/shard_map/ppermute | solution.py:443
  78.4 0.9 %collective-permute-done.1.got_ref = f32[128,128]{1,0:T(8,128)S(1)} collective-permute-done((f32[128,128]{1,0:T(8,128)S(1)}, f32[128,128]{1,0:T(8,128)S(1)}, u32[]{:S(2)}, u32[]{:S(2)}) %collective-permute-start.1) | collective-permute-done | bytes 65568 | tf_op jit(solution)/shard_map/ppermute | solution.py:443
  79.3 0.6 last.1
  (5 shorter events, 0.0 us)
Async XLA Ops:
  0.0 7.1 %copy-start.2 = (s32[16,10]{1,0:T(8,128)S(1)}, s32[16,10]{1,0:T(8,128)}, u32[]{:S(2)}) copy-start(s32[16,10]{1,0:T(8,128)} %param.31) | copy-start | bytes 1924
  0.0 8.1 %copy-start.1 = (f32[2048]{0:T(1024)S(1)}, f32[2048]{0:T(1024)}, u32[]{:S(2)}) copy-start(f32[2048]{0:T(1024)} %param.30) | copy-start | bytes 24580
  5.6 2.5 %collective-permute-start = (f32[256,128]{1,0:T(8,128)S(1)}, f32[256,128]{1,0:T(8,128)S(1)}, u32[]{:S(2)}, u32[]{:S(2)}) collective-permute-start(f32[256,128]{1,0:T(8,128)S(1)} %delta.1.own_ref), channel_id=1, source_target_pairs={{0,64},{64,0},{1,65},{65,1},{2,66},{66,2},{3,67},{67,3},{4,68},{68... | collective-permute-start | bytes 393224 | tf_op jit(solution)/shard_map/ppermute | solution.py:432
  7.3 32.8 %copy-start = (bf16[2,2048,512]{2,1,0:T(8,128)(2,1)S(1)}, bf16[2,2048,512]{2,1,0:T(8,128)(2,1)}, u32[]{:S(2)}) copy-start(bf16[2,2048,512]{2,1,0:T(8,128)(2,1)} %gate_ref.1) | copy-start | bytes 12582916
  40.2 16.8 %copy-start.3 = (f32[16,10]{1,0:T(8,128)S(1)}, f32[16,10]{1,0:T(8,128)}, u32[]{:S(2)}) copy-start(f32[16,10]{1,0:T(8,128)} %param.32) | copy-start | bytes 1924
  46.9 27.6 %all-to-all-start.1 = ((bf16[64,96,128]{2,1,0:T(8,128)(2,1)}), bf16[64,96,128]{2,1,0:T(8,128)(2,1)S(1)}, u32[]{:S(2)}, u32[]{:S(2)}) async-start(bf16[64,96,128]{2,1,0:T(8,128)(2,1)} %experts.1), calls=%async_computation.1 | async-start | bytes 3145728 | tf_op jit(solution)/shard_map/all_to_all | solution.py:380
  75.3 4.0 %collective-permute-start.1 = (f32[128,128]{1,0:T(8,128)S(1)}, f32[128,128]{1,0:T(8,128)S(1)}, u32[]{:S(2)}, u32[]{:S(2)}) collective-permute-start(f32[128,128]{1,0:T(8,128)S(1)} %get-tuple-element.8), channel_id=1, source_target_pairs={{0,64},{64,0},{1,65},{65,1},{2,66},{66,2},{3,67},{67,3},{4,68},{68... | collective-permute-start | bytes 196616 | tf_op jit(solution)/shard_map/ppermute | solution.py:443

commit v4 on v3

--- a/solution.py
+++ b/solution.py
@@ -294,66 +294,82 @@
     )(received, w_gate, *in_hbm(w_up, w_down))
 
 
-def gather_kernel(side_ref, slot_ref, weight_ref, back_ref, keep_ref, send_ref, sums_ref):
-    blocks = sums_ref.shape[0]
+def half_sums(take_high, slot_ref, weight_ref, back_ref, tokens, blocks, store):
     half = blocks // 2
-    tokens = keep_ref.shape[0] // half
     top = slot_ref.shape[0] // tokens
-    side = side_ref[0]
     for t in range(tokens):
-        total = jnp.zeros((blocks, LANES), jnp.float32)
+        total = jnp.zeros((half, LANES), jnp.float32)
         for k in range(top):
             at = pl.multiple_of(slot_ref[t * top + k] * blocks, blocks)
             tile = back_ref[pl.ds(at, blocks), :].astype(jnp.float32)
+            tile = jnp.where(take_high, tile[half:], tile[:half])
             total = total + weight_ref[t * top + k] * tile
-        sums_ref[...] = total
-        own = pl.multiple_of(side * half, half)
-        other = pl.multiple_of((1 - side) * half, half)
-        keep_ref[t * half : (t + 1) * half, :] = sums_ref[pl.ds(own, half), :]
-        send_ref[t * half : (t + 1) * half, :] = sums_ref[pl.ds(other, half), :]
-
-
-def gather_call(side, slots, weights, back, tokens, blocks):
+        store(t, total)
+
+
+def send_kernel(side_ref, slot_ref, weight_ref, back_ref, out_ref, *, blocks):
+    half = blocks // 2
+
+    def store(t, total):
+        out_ref[t * half : (t + 1) * half, :] = total
+
+    tokens = out_ref.shape[0] // half
+    half_sums(side_ref[0] == 0, slot_ref, weight_ref, back_ref, tokens, blocks, store)
+
+
+def keep_kernel(side_ref, slot_ref, weight_ref, back_ref, own_ref, other_ref, out_ref, *, blocks):
+    half = blocks // 2
+    side = side_ref[0]
+
+    def store(t, total):
+        at = pl.multiple_of((2 * t + side) * half, half)
+        hidden = own_ref[pl.ds(at, half), :] + other_ref[pl.ds(at, half), :]
+        out_ref[t * half : (t + 1) * half, :] = hidden + total
+
+    tokens = out_ref.shape[0] // half
+    half_sums(side == 1, slot_ref, weight_ref, back_ref, tokens, blocks, store)
+
+
+def half_call(kernel, name, side, slots, weights, back, *hidden, tokens, blocks):
     vmem = pl.BlockSpec(memory_space=pltpu.VMEM)
     smem = pl.BlockSpec(memory_space=pltpu.SMEM)
-    half = jax.ShapeDtypeStruct((tokens * blocks // 2, LANES), jnp.float32)
+    entries = slots.shape[0]
     return pl.pallas_call(
-        gather_kernel,
-        out_shape=(half, half),
-        in_specs=[smem, smem, smem, vmem],
-        out_specs=(vmem, vmem),
-        scratch_shapes=[pltpu.VMEM((blocks, LANES), jnp.float32)],
+        lambda *refs: kernel(*refs, blocks=blocks),
+        out_shape=jax.ShapeDtypeStruct((tokens * blocks // 2, LANES), jnp.float32),
+        in_specs=[smem, smem, smem, vmem] + [vmem] * len(hidden),
+        out_specs=vmem,
         compiler_params=pltpu.CompilerParams(vmem_limit_bytes=16 * MIB),
-        name="combine",
-    )(side, slots, weights, back)
-
-
-def last_kernel(side_ref, own_ref, other_ref, keep_ref, got_ref, out_ref, sums_ref):
+        cost_estimate=pl.CostEstimate(
+            flops=2 * entries * blocks * LANES,
+            bytes_accessed=2 * entries * blocks * LANES,
+            transcendentals=0,
+        ),
+        name=name,
+    )(side, slots, weights, back, *hidden)
+
+
+def last_kernel(keep_ref, got_ref, out_ref, sums_ref):
     tokens, width = out_ref.shape
     half = width // LANES
-    side = side_ref[0]
-    for t in range(tokens):
-        at = pl.multiple_of((2 * t + side) * half, half)
-        rows = slice(t * half, (t + 1) * half)
-        hidden = own_ref[pl.ds(at, half), :] + other_ref[pl.ds(at, half), :]
-        sums_ref[rows, :] = hidden + (keep_ref[rows, :] + got_ref[rows, :])
+    sums_ref[...] = keep_ref[...] + got_ref[...]
     for f in range(half):
         out_ref[:, f * LANES : (f + 1) * LANES] = sums_ref[
             pl.ds(f, tokens, stride=half), :
         ].astype(jnp.bfloat16)
 
 
-def last_call(side, own, other, keep, got, tokens):
+def last_call(keep, got, tokens):
     vmem = pl.BlockSpec(memory_space=pltpu.VMEM)
     return pl.pallas_call(
         last_kernel,
         out_shape=jax.ShapeDtypeStruct((tokens, keep.size // tokens), jnp.bfloat16),
-        in_specs=[pl.BlockSpec(memory_space=pltpu.SMEM), vmem, vmem, vmem, vmem],
+        in_specs=[vmem, vmem],
         out_specs=vmem,
         scratch_shapes=[pltpu.VMEM(keep.shape, jnp.float32)],
         compiler_params=pltpu.CompilerParams(vmem_limit_bytes=16 * MIB),
         name="last",
-    )(side, own, other, keep, got)
+    )(keep, got)
 
 
 def slot_tables(route_ids, route_weight, side_index, per_side, experts):
@@ -439,9 +455,11 @@
         received.reshape(dev_count, -1, LANES), w_gate, w_up, w_down
     ).reshape(received.shape)
     back = exchange(expert_out, dev_count)
-    keep, send = gather_call(side, slots, weights, back, tokens, blocks)
+    sizes = dict(tokens=tokens, blocks=blocks)
+    send = half_call(send_kernel, "send", side, slots, weights, back, **sizes)
     got = lax.ppermute(send, "side", swap)
-    return last_call(side, own, other, keep, got, tokens)
+    keep = half_call(keep_kernel, "keep", side, slots, weights, back, own, other, **sizes)
+    return last_call(keep, got, tokens)
 
 
 def solution(mesh):

time: 80.2 us -> 80.2 us (level)
    ppermute x1, waiting for transfers between devices: 0.9 us -> 0.08 us  [body(): got = lax.ppermute(send, 'side', swap)]
    pallas_call x1 -> x2, Pallas kernels: 0.85 us -> 1.64 us  [half_call(): pl.pallas_call(lambda *refs: kernel(*refs, blocks=blocks), out_shape=jax....]
  transfers between devices with their start and end apart: 3 -> 3, of which waited for: 3 -> 3; matrix products, arithmetic and copies ran while one was open for 1% -> 1% of each run, Pallas kernels for 0% -> 1%
where the time goes in v4:
time: 80.2 us; the launch traced here: 79.9 us
  blocking collectives  30.9 us (39%)
  waiting for transfers between devices  17.9 us (22%)
  Pallas kernels  15.8 us (20%)
  starting transfers between devices  14.6 us (18%)
    all_to_all x1, blocking collectives, exchange(): lax.all_to_all(rows, ('side', 'dev'), split_axis=0, concat_axis=0, axis_i...  30.9 us
    all_to_all x1, waiting for transfers between devices, exchange(): lax.all_to_all(rows, ('side', 'dev'), split_axis=0, concat_axis=0, axis_i...  17.4 us
    all_to_all x1, starting transfers between devices, exchange(): lax.all_to_all(rows, ('side', 'dev'), split_axis=0, concat_axis=0, axis_i...  10.1 us
    pallas_call x1, Pallas kernels, expert_call(): pl.pallas_call(expert_kernel, out_shape=jax.ShapeDtypeStruct(received.sha...  6.72 us
    pallas_call x1, Pallas kernels, delta_call(): pl.pallas_call(delta_kernel, out_shape=jax.ShapeDtypeStruct((tokens * wid...  5.62 us
    ppermute x1, starting transfers between devices, body(): got = lax.ppermute(send, 'side', swap)  3.05 us
    pallas_call x2, Pallas kernels, half_call(): pl.pallas_call(lambda *refs: kernel(*refs, blocks=blocks), out_shape=jax....  1.64 us
  transfers between devices with their start and end apart: 3, of which 3 were waited for; matrix products, arithmetic and copies ran while one was open for 1% of the time, Pallas kernels for 1%

profile of v4, /device:TPU:1, one launch (start us, length us, event | category | flops | bytes accessed | tf_op | source)
XLA Modules:
  0.0 79.9 jit_solution(13216993614716971342)
XLA Ops:
  0.0 0.0 copy-start.2
  0.0 0.0 copy-start.1
  0.0 5.6 %delta.1.own_ref.refs_4_ = f32[256,128]{1,0:T(8,128)S(1)} custom-call(s32[1]{0:T(128)} %bitcast.side_ref.refs_0_, bf16[16,4,128]{2,1,0:T(4,128)(2,1)} %refs_0_.1, bf16[16,4,128]{2,1,0:T(4,128)(2,1)} %refs_1_.1, bf16[16,8,128]{2,1,0:T(8,128)(2,1)} %refs_2_.1, bf16[16,8,128]{2,1,0:T(8,128)(2,1)} %refs_3_.1, f32[8,16]{1,0:T(8,128)} %bitcast.13, ...), custom_call_target="tpu_custom_call" | custom-call | tf_op jit(solution)/shard_map/delta/pallas_call | solution.py:144
  5.6 1.5 %collective-permute-start = (f32[256,128]{1,0:T(8,128)S(1)}, f32[256,128]{1,0:T(8,128)S(1)}, u32[]{:S(2)}, u32[]{:S(2)}) collective-permute-start(f32[256,128]{1,0:T(8,128)S(1)} %delta.1.own_ref.refs_4_), channel_id=1, source_target_pairs={{0,64},{64,0},{1,65},{65,1},{2,66},{66,2},{3,67},{67,3},{4,68},{68... | collective-permute-start | bytes 393224 | tf_op jit(solution)/shard_map/ppermute | solution.py:448
  7.1 0.0 copy-done.2
  7.1 0.1 reshape.84
  7.2 0.1 gt.17
  7.3 0.0 copy-start
  7.3 0.2 convert_reduce_fusion
  7.6 0.1 select_reduce_fusion
  7.7 0.4 collective-permute-done.other_ref.refs_5_
  8.1 0.0 copy-done.1
  8.1 1.1 %pack.1 = bf16[6144,128]{1,0:T(8,128)(2,1)S(1)} custom-call(s32[384]{0:T(512)S(1)} %broadcast_subtract_fusion.source_ref, f32[256,128]{1,0:T(8,128)S(1)} %delta.1.own_ref.refs_4_, f32[256,128]{1,0:T(8,128)S(1)} %collective-permute-done.other_ref.refs_5_, f32[16,128]{1,0:T(8,128)S(1)} %bitcast.12), custom_call_target="tpu_custom_call" | custom-call | tf_op jit(solution)/shard_map/pack/pallas_call | solution.py:189
  9.3 30.9 %all_to_all.17.x_ref = bf16[64,96,128]{2,1,0:T(8,128)(2,1)S(1)} all-to-all(bf16[64,96,128]{2,1,0:T(8,128)(2,1)S(1)} %bitcast.11), channel_id=1, replica_groups={{0,1,2,3,4,5,6,7,8,9,10,11,12,13,14,15,16,17,18,19,20,21,22,23,24,25,26..., dimensions={0} | all-to-all | bytes 3145728 | tf_op jit(solution)/shard_map/all_to_all | solution.py:396
  40.2 0.0 copy-done
  40.2 0.0 copy-start.3
  40.2 6.7 %experts.1 = bf16[64,96,128]{2,1,0:T(8,128)(2,1)} custom-call(bf16[64,96,128]{2,1,0:T(8,128)(2,1)S(1)} %all_to_all.17.x_ref, bf16[2,2048,512]{2,1,0:T(8,128)(2,1)S(1)} %copy-done, bf16[2,2048,512]{2,1,0:T(8,128)(2,1)} %up_hbm.1, bf16[2,512,2048]{2,1,0:T(8,128)(2,1)} %down_hbm.1), custom_call_target="tpu_custom_call" | custom-call | tf_op jit(solution)/shard_map/experts/pallas_call | solution.py:281
  46.9 10.1 %all-to-all-start.1 = ((bf16[64,96,128]{2,1,0:T(8,128)(2,1)}), bf16[64,96,128]{2,1,0:T(8,128)(2,1)S(1)}, u32[]{:S(2)}, u32[]{:S(2)}) async-start(bf16[64,96,128]{2,1,0:T(8,128)(2,1)} %experts.1), calls=%async_computation.1 | async-start | bytes 3145728 | tf_op jit(solution)/shard_map/all_to_all | solution.py:396
  57.0 0.0 copy-done.3
  57.0 0.1 reshape.85
  57.1 17.4 %all-to-all-done.1 = bf16[64,96,128]{2,1,0:T(8,128)(2,1)S(1)} async-done(((bf16[64,96,128]{2,1,0:T(8,128)(2,1)}), bf16[64,96,128]{2,1,0:T(8,128)(2,1)S(1)}, u32[]{:S(2)}, u32[]{:S(2)}) %all-to-all-start.1) | async-done | bytes 1572896 | tf_op jit(solution)/shard_map/all_to_all | solution.py:396
  74.5 0.8 %send.1 = f32[128,128]{1,0:T(8,128)S(1)} custom-call(s32[1]{0:T(128)} %bitcast.side_ref.refs_0_, s32[160]{0:T(256)S(1)} %get-tuple-element.5.refs_1_, f32[160]{0:T(256)S(1)} %broadcast_select_fusion.refs_2_, bf16[6144,128]{1,0:T(8,128)(2,1)S(1)} %bitcast.9), custom_call_target="tpu_custom_call" | custom-call | flops 655360 | bytes 655360 | tf_op jit(solution)/shard_map/send/pallas_call | solution.py:337
  75.3 3.0 %collective-permute-start.1 = (f32[128,128]{1,0:T(8,128)S(1)}, f32[128,128]{1,0:T(8,128)S(1)}, u32[]{:S(2)}, u32[]{:S(2)}) collective-permute-start(f32[128,128]{1,0:T(8,128)S(1)} %send.1), channel_id=1, source_target_pairs={{0,64},{64,0},{1,65},{65,1},{2,66},{66,2},{3,67},{67,3},{4,68},{68... | collective-permute-start | bytes 196616 | tf_op jit(solution)/shard_map/ppermute | solution.py:460
  78.4 0.8 %keep.1.keep_ref = f32[128,128]{1,0:T(8,128)S(1)} custom-call(s32[1]{0:T(128)} %bitcast.side_ref.refs_0_, s32[160]{0:T(256)S(1)} %get-tuple-element.5.refs_1_, f32[160]{0:T(256)S(1)} %broadcast_select_fusion.refs_2_, bf16[6144,128]{1,0:T(8,128)(2,1)S(1)} %bitcast.10, f32[256,128]{1,0:T(8,128)S(1)} %delta.1.own_ref.refs_4_, ...), custom_call_target="tpu_custom_call" | custom-call | flops 655360 | bytes 655360 | tf_op jit(solution)/shard_map/keep/pallas_call | solution.py:337
  79.2 0.1 collective-permute-done.1.got_ref
  79.3 0.6 last.1
  (5 shorter events, 0.0 us)
Async XLA Ops:
  0.0 7.1 %copy-start.2 = (s32[16,10]{1,0:T(8,128)S(1)}, s32[16,10]{1,0:T(8,128)}, u32[]{:S(2)}) copy-start(s32[16,10]{1,0:T(8,128)} %param.31) | copy-start | bytes 1924
  0.0 8.1 %copy-start.1 = (f32[2048]{0:T(1024)S(1)}, f32[2048]{0:T(1024)}, u32[]{:S(2)}) copy-start(f32[2048]{0:T(1024)} %param.30) | copy-start | bytes 24580
  5.6 2.5 %collective-permute-start = (f32[256,128]{1,0:T(8,128)S(1)}, f32[256,128]{1,0:T(8,128)S(1)}, u32[]{:S(2)}, u32[]{:S(2)}) collective-permute-start(f32[256,128]{1,0:T(8,128)S(1)} %delta.1.own_ref.refs_4_), channel_id=1, source_target_pairs={{0,64},{64,0},{1,65},{65,1},{2,66},{66,2},{3,67},{67,3},{4,68},{68... | collective-permute-start | bytes 393224 | tf_op jit(solution)/shard_map/ppermute | solution.py:448
  7.3 32.8 %copy-start = (bf16[2,2048,512]{2,1,0:T(8,128)(2,1)S(1)}, bf16[2,2048,512]{2,1,0:T(8,128)(2,1)}, u32[]{:S(2)}) copy-start(bf16[2,2048,512]{2,1,0:T(8,128)(2,1)} %gate_ref.1) | copy-start | bytes 12582916
  40.2 16.8 %copy-start.3 = (f32[16,10]{1,0:T(8,128)S(1)}, f32[16,10]{1,0:T(8,128)}, u32[]{:S(2)}) copy-start(f32[16,10]{1,0:T(8,128)} %param.32) | copy-start | bytes 1924
  46.9 27.6 %all-to-all-start.1 = ((bf16[64,96,128]{2,1,0:T(8,128)(2,1)}), bf16[64,96,128]{2,1,0:T(8,128)(2,1)S(1)}, u32[]{:S(2)}, u32[]{:S(2)}) async-start(bf16[64,96,128]{2,1,0:T(8,128)(2,1)} %experts.1), calls=%async_computation.1 | async-start | bytes 3145728 | tf_op jit(solution)/shard_map/all_to_all | solution.py:396
  75.3 3.9 %collective-permute-start.1 = (f32[128,128]{1,0:T(8,128)S(1)}, f32[128,128]{1,0:T(8,128)S(1)}, u32[]{:S(2)}, u32[]{:S(2)}) collective-permute-start(f32[128,128]{1,0:T(8,128)S(1)} %send.1), channel_id=1, source_target_pairs={{0,64},{64,0},{1,65},{65,1},{2,66},{66,2},{3,67},{67,3},{4,68},{68... | collective-permute-start | bytes 196616 | tf_op jit(solution)/shard_map/ppermute | solution.py:460
